TPU v7x, 256 devices: a whole 4x4x8 slice. The times are simulated.
256 devices in a mesh: seq: 64 (over z, y, core), mp: 4 (over x).
Axes of the slice: x: 4, y: 4, z: 8, core: 2. Of those that a mesh axis runs over, the one named last changes fastest.
Arguments:
- residual: bfloat16 [8192, 8192], P('seq', 'mp'), may hold values from -6 to 6
- chosen_pos: int32 [3072], P('seq'), may hold values from 0 to 127, as said below
- chosen_count: int32 [64], P('seq'), may hold values from 0 to 48, as said below
- router_weight: float32 [8192], P('mp'), may hold values from -0.0625 to 0.0625
- weight_in: bfloat16 [8192, 53248], P('mp', 'seq')
- weight_out: bfloat16 [22528, 8192], P('seq', 'mp'), may hold values from -0.0390625 to 0.0390625
- cotangent: bfloat16 [8192, 8192], P('seq', 'mp'), may hold values from -6 to 6
Outputs:
- output: bfloat16 [8192, 8192], P('seq', 'mp')
- grad_residual: bfloat16 [8192, 8192], P('seq', 'mp')
Inputs may be any that keep to these rules, and one draw needn't show every extreme that they name: `chosen_count`: in each aligned window of 4 consecutive sequence shards the counts sum to exactly 64; some shard holds 48. `chosen_pos`: in shard s's block, the first chosen_count[s] entries are distinct increasing local positions; the remaining entries are 0.
All inputs are finite; a program needn't handle non-finite values.
Results may differ from a plain program's by a relative error of at most 0.01.
Values may be sent and summed in bfloat16 or wider, within the bound.
A program may use at most 64 MiB of HBM per device.

v0:
```python
import jax
import jax.numpy as jnp
from jax import lax
from jax.sharding import PartitionSpec as P

D = 8192
HS = 128
GROUP = 4


def entering(part, axis, combine, identity):
    place = lax.axis_index(axis)
    gathered = lax.all_gather(part, axis)
    state = jnp.zeros_like(part) + jnp.asarray(identity, part.dtype)

    def one(hop, state):
        return combine(state, lax.dynamic_index_in_dim(gathered, hop, 0, False))

    return lax.fori_loop(0, place, one, state)


def shifted(value, axis, steps):
    count = lax.axis_size(axis)
    first, last = (max(0, -steps), min(count, count - steps))
    return lax.ppermute(value, axis, [(source, source + steps) for source in range(first, last)])


def norm_rows(values, epsilon):
    scale = lax.rsqrt(jnp.mean(values * values, axis=-1, keepdims=True) + epsilon)
    return (values * scale, scale)


def norm_back(values, scale, grads):
    return scale * grads - values * scale**3 * jnp.mean(grads * values, axis=-1, keepdims=True)


def gather_rows(block):
    return lax.all_gather(block, "seq", axis=0, tiled=True)


def add_counts(earlier, later):
    return earlier + later


def exp_scores(query_b, key_block, query_order, key_order):
    raw = lax.dot_general(
        query_b, key_block[:, :HS], (((1,), (1,)), ((), ())), preferred_element_type=jnp.float32
    )
    visible = key_order[None, :] <= query_order[:, None]
    return jnp.where(visible, jnp.exp(raw * HS ** (-0.5)), jnp.float32(0.0))


def local(residual, chosen_pos, chosen_count, router_weight, weight_in, weight_out, cotangent):
    seq_index = lax.axis_index("seq")
    mp_index = lax.axis_index("mp")
    chosen = chosen_count[0]
    maxsrc = chosen_pos.shape[0]
    tok_dev = residual.shape[0]
    capacity = maxsrc // 3
    total_rows = capacity * lax.axis_size("seq")
    block_rows = total_rows // lax.axis_size("mp")
    factor = HS ** (-0.5)
    reach = GROUP - 2
    slot_ids = jnp.arange(maxsrc, dtype=jnp.int32)
    is_valid = slot_ids < chosen
    rows_src = residual[chosen_pos]
    router_logit = lax.psum(jnp.sum(rows_src.astype(jnp.float32) * router_weight, axis=-1), "mp")
    gate_value = jax.nn.sigmoid(router_logit)
    before = entering(chosen_count, "seq", add_counts, jnp.zeros((1,), jnp.int32))[0]
    target = before + slot_ids
    owner_shard = target // capacity
    slot_of = target % capacity
    cell_ids = jnp.arange(capacity, dtype=jnp.int32)

    def route_in(row_block):
        summed = jnp.zeros((capacity, row_block.shape[1]), jnp.float32)
        for offset in range(-reach, reach + 1):
            chosen_here = (owner_shard == seq_index + offset) & is_valid
            selector = ((slot_of[None, :] == cell_ids[:, None]) & chosen_here[None, :]).astype(
                jnp.bfloat16
            )
            moved_block = jnp.dot(selector, row_block, preferred_element_type=jnp.float32).astype(
                jnp.bfloat16
            )
            if offset != 0:
                moved_block = shifted(moved_block, "seq", offset)
            summed = summed + moved_block.astype(jnp.float32)
        return summed.astype(jnp.bfloat16)

    def route_out(row_block):
        summed = jnp.zeros((maxsrc, row_block.shape[1]), jnp.float32)
        for offset in range(-reach, reach + 1):
            chosen_here = (owner_shard == seq_index + offset) & is_valid
            selector = ((slot_of[:, None] == cell_ids[None, :]) & chosen_here[:, None]).astype(
                jnp.bfloat16
            )
            moved_block = row_block
            if offset != 0:
                moved_block = shifted(row_block, "seq", -offset)
            summed = summed + jnp.dot(selector, moved_block, preferred_element_type=jnp.float32)
        return summed.astype(jnp.bfloat16)

    compact = route_in(rows_src)
    own_rows = compact.astype(jnp.float32)
    square_sum = lax.psum(jnp.sum(own_rows * own_rows, axis=-1), "mp")
    in_scale = lax.rsqrt(square_sum / D + 1e-05)[:, None]
    normed_all = gather_rows((own_rows * in_scale).astype(jnp.bfloat16))
    piece = normed_all
    project = lax.psum_scatter(
        jnp.dot(piece, weight_in, preferred_element_type=jnp.float32).astype(jnp.bfloat16),
        "mp",
        scatter_dimension=0,
        tiled=True,
    ).astype(jnp.float32)
    ffd = (project.shape[1] - 3 * HS) // 2
    query = project[:, :HS]
    keyraw = project[:, HS : 2 * HS]
    gate_in = project[:, 3 * HS : 3 * HS + ffd]
    up_in = project[:, 3 * HS + ffd :]
    query_n, query_scale = norm_rows(query, 1e-06)
    key_n, key_scale = norm_rows(keyraw, 1e-06)
    query_b = query_n.astype(jnp.bfloat16)
    keys_b = jnp.concatenate(
        [key_n.astype(jnp.bfloat16), project[:, 2 * HS : 3 * HS].astype(jnp.bfloat16)], axis=-1
    )
    query_order = mp_index * block_rows + jnp.arange(block_rows, dtype=jnp.int32)
    key_order_all = jnp.arange(total_rows, dtype=jnp.int32)
    piece = lax.all_gather(keys_b, "mp", axis=0, tiled=True)
    key_order = jnp.arange(piece.shape[0], dtype=jnp.int32)
    expo = exp_scores(query_b, piece, query_order, key_order)
    denom = jnp.sum(expo, axis=-1)
    accum = jnp.dot(expo.astype(jnp.bfloat16), piece[:, HS:], preferred_element_type=jnp.float32)
    attended = (accum / denom[:, None]).astype(jnp.bfloat16)
    sigma = jax.nn.sigmoid(gate_in)
    hidden = (gate_in * sigma * up_in).astype(jnp.bfloat16)
    joined = jnp.concatenate([attended, hidden], axis=-1)
    joined_all = lax.all_gather(joined, "mp", axis=0, tiled=True)
    piece = joined_all
    delta_compact = lax.psum_scatter(
        jnp.dot(piece, weight_out, preferred_element_type=jnp.float32),
        "seq",
        scatter_dimension=0,
        tiled=True,
    ).astype(jnp.bfloat16)
    delta_src = route_out(delta_compact)
    out_rows = (
        rows_src.astype(jnp.float32) + gate_value[:, None] * delta_src.astype(jnp.float32)
    ).astype(jnp.bfloat16)
    target_rows = jnp.where(is_valid, chosen_pos, tok_dev)
    output = residual.at[target_rows].set(out_rows, mode="drop")
    grad_rows = cotangent[chosen_pos]
    grad_f = grad_rows.astype(jnp.float32)
    dgate = lax.psum(jnp.sum(grad_f * delta_src.astype(jnp.float32), axis=-1), "mp")
    dlogit = dgate * gate_value * (1.0 - gate_value)
    ddelta_src = jnp.where(
        is_valid[:, None], gate_value[:, None] * grad_f, jnp.float32(0.0)
    ).astype(jnp.bfloat16)
    ddelta_all = gather_rows(route_in(ddelta_src))
    piece = ddelta_all
    djoined = lax.psum_scatter(
        lax.dot_general(
            piece, weight_out, (((1,), (1,)), ((), ())), preferred_element_type=jnp.float32
        ).astype(jnp.bfloat16),
        "mp",
        scatter_dimension=0,
        tiled=True,
    ).astype(jnp.float32)
    dattended = djoined[:, :HS].astype(jnp.bfloat16)
    dhidden = djoined[:, HS:]
    dup = (dhidden * gate_in * sigma).astype(jnp.bfloat16)
    dgate_in = (dhidden * up_in * sigma * (1.0 + gate_in * (1.0 - sigma))).astype(jnp.bfloat16)
    all_keys = lax.all_gather(keys_b, "mp", axis=0, tiled=True)
    back_expo = exp_scores(query_b, all_keys, query_order, key_order_all)
    prob = back_expo / denom[:, None]
    dprob = lax.dot_general(
        dattended, all_keys[:, HS:], (((1,), (1,)), ((), ())), preferred_element_type=jnp.float32
    )
    inner = jnp.sum(prob * dprob, axis=-1)
    dscore = (prob * (dprob - inner[:, None])).astype(jnp.bfloat16)
    prob_b = prob.astype(jnp.bfloat16)
    dquery_n = jnp.dot(dscore, all_keys[:, :HS], preferred_element_type=jnp.float32) * factor
    dkey_part = (
        lax.dot_general(
            dscore, query_b, (((0,), (0,)), ((), ())), preferred_element_type=jnp.float32
        )
        * factor
    )
    dvalue_part = lax.dot_general(
        prob_b, dattended, (((0,), (0,)), ((), ())), preferred_element_type=jnp.float32
    )
    key_grad = lax.psum_scatter(
        jnp.concatenate([dkey_part, dvalue_part], axis=-1).astype(jnp.bfloat16),
        "mp",
        scatter_dimension=0,
        tiled=True,
    ).astype(jnp.float32)
    dquery = norm_back(query, query_scale, dquery_n).astype(jnp.bfloat16)
    dkey = norm_back(keyraw, key_scale, key_grad[:, :HS]).astype(jnp.bfloat16)
    dvalue = key_grad[:, HS:].astype(jnp.bfloat16)
    dproject = jnp.concatenate([dquery, dkey, dvalue, dgate_in, dup], axis=-1)
    dproject_all = lax.all_gather(dproject, "mp", axis=0, tiled=True)
    piece = dproject_all
    dnormed = lax.psum_scatter(
        lax.dot_general(
            piece, weight_in, (((1,), (1,)), ((), ())), preferred_element_type=jnp.float32
        ),
        "seq",
        scatter_dimension=0,
        tiled=True,
    )
    inner_norm = lax.psum(jnp.sum(dnormed * own_rows, axis=-1), "mp") / D
    dinput = (in_scale * dnormed - own_rows * in_scale**3 * inner_norm[:, None]).astype(
        jnp.bfloat16
    )
    dinput_src = route_out(dinput)
    grad_src = (grad_f + dinput_src.astype(jnp.float32) + dlogit[:, None] * router_weight).astype(
        jnp.bfloat16
    )
    grad_residual = cotangent.at[target_rows].set(grad_src, mode="drop")
    return (output, grad_residual)


def solution(mesh):
    return jax.shard_map(
        local,
        mesh=mesh,
        in_specs=(
            P("seq", "mp"),
            P("seq"),
            P("seq"),
            P("mp"),
            P("mp", "seq"),
            P("seq", "mp"),
            P("seq", "mp"),
        ),
        out_specs=(P("seq", "mp"), P("seq", "mp")),
        check_vma=False,
    )
```

profile of v0, /device:TPU:1, one launch (start us, length us, event | category | flops | bytes accessed | tf_op | source)
XLA Modules:
  0.0 860.2 jit_solution(8977198311392047479)
XLA Ops:
  13.7 20.7 %all-reduce = s32[64]{0:T(128)S(1)} all-reduce(s32[64]{0:T(128)S(1)} %dynamic-update-slice), channel_id=2, replica_groups=mesh['seq'=64,'mp'=4] {'seq'}, use_global_device_ids=true, to_apply=%add | all-reduce | flops 64 | bytes 512
  44.9 5.3 collective-permute-start.1
  52.5 5.0 collective-permute-start.2
  59.1 4.6 collective-permute-start.3
  67.9 8.6 all-reduce.2
  77.2 147.1 %all-gather.5.cloned.1.call-done = bf16[1024,2048]{1,0:T(8,128)(2,1)} async-done(((bf16[16,2048]{1,0:T(8,128)(2,1)}), bf16[1024,2048]{1,0:T(8,128)(2,1)}) %all-gather.5.cloned.1.call-update) | async-done | bytes 4194320 | tf_op jit(solution)/shard_map/all_gather | solution.py:38
  224.4 7.0 convolution_convert_fusion.10
  231.5 25.9 %reduce-scatter.6.cloned.1.call-done = bf16[256,832]{0,1:T(8,128)(2,1)} async-done(((bf16[1024,832]{0,1:T(8,128)(2,1)}), bf16[256,832]{0,1:T(8,128)(2,1)}) %reduce-scatter.6.cloned.1.call-update) | async-done | bytes 426000 | tf_op jit(solution)/shard_map/reduce_scatter | solution.py:109
  259.8 10.0 %all_gather.25 = bf16[1024,256]{0,1:T(8,128)(2,1)S(1)} all-gather(bf16[256,256]{0,1:T(8,128)(2,1)S(1)} %pad_maximum_fusion.2), channel_id=1, replica_groups=mesh['seq'=64,'mp'=4] {'mp'}, dimensions={0}, use_global_device_ids=true | all-gather | bytes 655360 | tf_op jit(solution)/shard_map/all_gather | solution.py:128
  271.7 10.9 %all_gather.26 = bf16[1024,352]{0,1:T(8,128)(2,1)S(1)} all-gather(bf16[256,352]{0,1:T(8,128)(2,1)S(1)} %pad_maximum_fusion.1), channel_id=1, replica_groups=mesh['seq'=64,'mp'=4] {'mp'}, dimensions={0}, use_global_device_ids=true | all-gather | bytes 901120 | tf_op jit(solution)/shard_map/all_gather | solution.py:137
  282.6 5.6 fusion.134
  291.2 150.3 %reduce-scatter.8.cloned.1.call-done = f32[16,2048]{1,0:T(8,128)} async-done(((f32[1024,2048]{1,0:T(8,128)}), f32[16,2048]{1,0:T(8,128)}) %reduce-scatter.8.cloned.1.call-update) | async-done | bytes 131088 | tf_op jit(solution)/shard_map/reduce_scatter | solution.py:139
  442.3 7.5 collective-permute-start.5
  465.2 3.5 collective-permute-start.11
  477.7 84.7 %all-gather.7.cloned.1.call-done = bf16[1024,2048]{1,0:T(8,128)(2,1)} async-done(((bf16[16,2048]{1,0:T(8,128)(2,1)}), bf16[1024,2048]{1,0:T(8,128)(2,1)}) %all-gather.7.cloned.1.call-update) | async-done | bytes 4194320 | tf_op jit(solution)/shard_map/all_gather | solution.py:38
  562.5 5.2 convolution_convert_fusion.11
  567.7 20.5 %reduce-scatter.10.cloned.1.call-done = bf16[256,352]{0,1:T(8,128)(2,1)} async-done(((bf16[1024,352]{0,1:T(8,128)(2,1)}), bf16[256,352]{0,1:T(8,128)(2,1)}) %reduce-scatter.10.cloned.1.call-update) | async-done | bytes 180240 | tf_op jit(solution)/shard_map/reduce_scatter | solution.py:160
  593.8 23.1 %reduce-scatter.12.cloned.1.call-done = bf16[256,256]{0,1:T(8,128)(2,1)} async-done(((bf16[1024,256]{0,1:T(8,128)(2,1)}), bf16[256,256]{0,1:T(8,128)(2,1)}) %reduce-scatter.12.cloned.1.call-update) | async-done | bytes 131088 | tf_op jit(solution)/shard_map/reduce_scatter | solution.py:191
  626.7 34.5 %all-gather.9.cloned.1.call-done = bf16[1024,832]{0,1:T(8,128)(2,1)} async-done(((bf16[256,832]{0,1:T(8,128)(2,1)}), bf16[1024,832]{0,1:T(8,128)(2,1)}) %all-gather.9.cloned.1.call-update) | async-done | bytes 1703952 | tf_op jit(solution)/shard_map/all_gather | solution.py:201
  661.2 8.2 fusion.135
  670.1 3.4 scatter_custom_fusion
  673.5 144.7 %reduce-scatter.14.cloned.1.call-done = f32[16,2048]{1,0:T(8,128)} async-done(((f32[1024,2048]{1,0:T(8,128)}), f32[16,2048]{1,0:T(8,128)}) %reduce-scatter.14.cloned.1.call-update) | async-done | bytes 131088 | tf_op jit(solution)/shard_map/reduce_scatter | solution.py:203
  819.2 8.4 all-reduce.1
  828.5 9.5 %collective-permute-start.13 = (bf16[16,2048]{1,0:T(8,128)(2,1)S(1)}, bf16[16,2048]{1,0:T(8,128)(2,1)S(1)}, u32[]{:S(2)}, u32[]{:S(2)}) collective-permute-start(bf16[16,2048]{1,0:T(8,128)(2,1)S(1)} %fusion.45), channel_id=1, source_target_pairs={{0,4},{4,8},{8,12},{12,16},{16,20},{20,24},{24,28},{28,32},{32,36}... | collective-permute-start | bytes 196616 | tf_op jit(solution)/shard_map/ppermute | solution.py:25
  (156 shorter events, 91.3 us)
Async XLA Ops:
  7.2 217.2 %all-gather.5.cloned.1.call-start = ((), (), s32[]{:S(2)}) async-start(), calls=%async_computation.5 | async-start | bytes 4259840 | tf_op jit(solution)/shard_map/all_gather | solution.py:38
  41.3 24.0 %collective-permute-start = (bf16[16,2048]{1,0:T(8,128)(2,1)}, bf16[16,2048]{1,0:T(8,128)(2,1)S(1)}, u32[]{:S(2)}, u32[]{:S(2)}) collective-permute-start(bf16[16,2048]{1,0:T(8,128)(2,1)} %convolution_convert_fusion.9), channel_id=1, source_target_pairs={{8,0},{12,4},{16,8},{20,12},{24,16},{28,20},{32,24},{36,28},{40,32... | collective-permute-start | bytes 196616 | tf_op jit(solution)/shard_map/ppermute | solution.py:25
  44.9 20.5 %collective-permute-start.1 = (bf16[16,2048]{1,0:T(8,128)(2,1)}, bf16[16,2048]{1,0:T(8,128)(2,1)S(1)}, u32[]{:S(2)}, u32[]{:S(2)}) collective-permute-start(bf16[16,2048]{1,0:T(8,128)(2,1)} %convolution_convert_fusion.8), channel_id=1, source_target_pairs={{4,0},{8,4},{12,8},{16,12},{20,16},{24,20},{28,24},{32,28},{36,32}... | collective-permute-start | bytes 196616 | tf_op jit(solution)/shard_map/ppermute | solution.py:25
  52.5 12.9 %collective-permute-start.2 = (bf16[16,2048]{1,0:T(8,128)(2,1)}, bf16[16,2048]{1,0:T(8,128)(2,1)}, u32[]{:S(2)}, u32[]{:S(2)}) collective-permute-start(bf16[16,2048]{1,0:T(8,128)(2,1)} %convolution_convert_fusion.6), channel_id=1, source_target_pairs={{0,4},{4,8},{8,12},{12,16},{16,20},{20,24},{24,28},{28,32},{32,36}... | collective-permute-start | bytes 196616 | tf_op jit(solution)/shard_map/ppermute | solution.py:25
  59.1 6.9 collective-permute-start.3
  77.2 180.2 %reduce-scatter.6.cloned.1.call-start = ((), (), s32[]{:S(2)}) async-start(), calls=%async_computation.6 | async-start | bytes 2129920 | tf_op jit(solution)/shard_map/reduce_scatter | solution.py:109
  231.4 210.0 %reduce-scatter.8.cloned.1.call-start = ((), (), s32[]{:S(2)}) async-start(), calls=%async_computation.7 | async-start | bytes 8519680 | tf_op jit(solution)/shard_map/reduce_scatter | solution.py:139
  288.3 274.2 %all-gather.7.cloned.1.call-start = ((), (), s32[]{:S(2)}) async-start(), calls=%async_computation.8 | async-start | bytes 4259840 | tf_op jit(solution)/shard_map/all_gather | solution.py:38
  442.3 14.1 %collective-permute-start.5 = (bf16[16,2048]{1,0:T(8,128)(2,1)S(1)}, bf16[16,2048]{1,0:T(8,128)(2,1)S(1)}, u32[]{:S(2)}, u32[]{:S(2)}) collective-permute-start(bf16[16,2048]{1,0:T(8,128)(2,1)S(1)} %convert_element_type.196), channel_id=1, source_target_pairs={{0,4},{4,8},{8,12},{12,16},{16,20},{20,24},{24,28},{28,32},{32,36}... | collective-permute-start | bytes 196616 | tf_op jit(solution)/shard_map/ppermute | solution.py:25
  450.1 6.6 collective-permute-start.4
  453.2 5.4 collective-permute-start.7
  454.5 5.6 collective-permute-start.6
  462.8 9.9 %collective-permute-start.10 = (bf16[16,2048]{1,0:T(8,128)(2,1)S(1)}, bf16[16,2048]{1,0:T(8,128)(2,1)S(1)}, u32[]{:S(2)}, u32[]{:S(2)}) collective-permute-start(bf16[16,2048]{1,0:T(8,128)(2,1)S(1)} %convolution_convert_fusion.1), channel_id=1, source_target_pairs={{0,4},{4,8},{8,12},{12,16},{16,20},{20,24},{24,28},{28,32},{32,36}... | collective-permute-start | bytes 196616 | tf_op jit(solution)/shard_map/ppermute | solution.py:25
  465.2 7.5 collective-permute-start.11
  468.7 6.8 collective-permute-start.8
  470.0 6.9 collective-permute-start.9
  477.7 110.5 %reduce-scatter.10.cloned.1.call-start = ((), (), s32[]{:S(2)}) async-start(), calls=%async_computation.9 | async-start | bytes 901120 | tf_op jit(solution)/shard_map/reduce_scatter | solution.py:160
  567.7 49.2 %reduce-scatter.12.cloned.1.call-start = ((), (), s32[]{:S(2)}) async-start(), calls=%async_computation.10 | async-start | bytes 655360 | tf_op jit(solution)/shard_map/reduce_scatter | solution.py:191
  593.6 67.6 %all-gather.9.cloned.1.call-start = ((), (), s32[]{:S(2)}) async-start(), calls=%async_computation.11 | async-start | bytes 2129920 | tf_op jit(solution)/shard_map/all_gather | solution.py:201
  626.7 191.4 %reduce-scatter.14.cloned.1.call-start = ((), (), s32[]{:S(2)}) async-start(), calls=%async_computation.12 | async-start | bytes 8519680 | tf_op jit(solution)/shard_map/reduce_scatter | solution.py:203
  828.5 16.1 %collective-permute-start.13 = (bf16[16,2048]{1,0:T(8,128)(2,1)S(1)}, bf16[16,2048]{1,0:T(8,128)(2,1)S(1)}, u32[]{:S(2)}, u32[]{:S(2)}) collective-permute-start(bf16[16,2048]{1,0:T(8,128)(2,1)S(1)} %fusion.45), channel_id=1, source_target_pairs={{0,4},{4,8},{8,12},{12,16},{16,20},{20,24},{24,28},{28,32},{32,36}... | collective-permute-start | bytes 196616 | tf_op jit(solution)/shard_map/ppermute | solution.py:25
  838.3 6.6 collective-permute-start.12
  841.4 5.4 collective-permute-start.15
  842.7 5.6 collective-permute-start.14
  (21 other events, 1389.4 us)
Sparse Core Ops, SparseCore 0:
  77.3 147.0 all-gather.4
  231.5 25.7 reduce-scatter.5
  288.4 152.9 reduce-scatter.7
  477.8 84.6 all-gather.6
  567.8 20.3 reduce-scatter.9
  593.7 23.1 reduce-scatter.11
  626.8 34.3 all-gather.8
  669.6 148.4 reduce-scatter.13
where the time goes:
time: 865 us; the launch traced here: 860 us
  waiting for transfers between devices  641 us (74%)
  blocking collectives  58.6 us (7%)
  starting transfers between devices  56.1 us (6%)
  matrix products  48 us (6%)
  local copies, waits for them, and re-layouts  21.7 us (3%)
  other arithmetic  19 us (2%)
  between operations  15.4 us (2%)
    all_gather x2, waiting for transfers between devices, gather_rows(): return lax.all_gather(block, 'seq', axis=0, tiled=True)  232 us
    reduce_scatter x1, waiting for transfers between devices, local(): lax.psum_scatter(jnp.dot(piece, weight_out, preferred_element_type=jnp.fl...  150 us
    reduce_scatter x1, waiting for transfers between devices, local(): lax.psum_scatter(lax.dot_general(piece, weight_in, (((1,), (1,)), ((), ()...  145 us
    ppermute x16, starting transfers between devices, shifted(): lax.ppermute(value, axis, [(source, source + steps) for source in range(f...  55.6 us
    all_gather x1, waiting for transfers between devices, local(): dproject_all = lax.all_gather(dproject, 'mp', axis=0, tiled=True)  34.5 us
    reduce_scatter x1, waiting for transfers between devices, local(): lax.psum_scatter(jnp.dot(piece, weight_in, preferred_element_type=jnp.flo...  25.9 us
    reduce_scatter x1, waiting for transfers between devices, local(): lax.psum_scatter(jnp.concatenate([dkey_part, dvalue_part], axis=-1).astyp...  23.1 us
    unnamed x1, blocking collectives  20.7 us
  transfers between devices with their start and end apart: 24, of which 14 were waited for; matrix products, arithmetic and copies ran while one was open for 2% of the time, Pallas kernels for 0%

commit v1 on v0

v1 whole, which is shorter than its diff:
```python
import functools

import jax
import jax.numpy as jnp
from jax import lax
from jax.experimental import pallas as pl
from jax.experimental.pallas import tpu as pltpu
from jax.sharding import PartitionSpec as P

MESH = pl.DeviceIdType.MESH
D = 8192
HS = 128
NZ, NY, NX = 8, 4, 4
CAP = 16
QD = D // NX
FFD = 224
WIN = 3 * HS + 2 * FFD
WINP = 896
WOUT = HS + FFD
WOUTP = 384
ROWS = 1024
BLK = 256
HALF = QD // 2
F32 = jnp.float32
BF16 = jnp.bfloat16
FACTOR = HS ** (-0.5)


def mod(value, n):
    return lax.rem(value + n, n)


def dot_nn(a, b):
    return jnp.dot(a, b, preferred_element_type=F32)


def dot_nt(a, b):
    return lax.dot_general(a, b, (((1,), (1,)), ((), ())), preferred_element_type=F32)


def dot_tn(a, b):
    return lax.dot_general(a, b, (((0,), (0,)), ((), ())), preferred_element_type=F32)


class Net:
    def __init__(self, send_sem, recv_sem):
        self.send_sem, self.recv_sem = send_sem, recv_sem
        self.used = 0
        self.sent = []
        seq = lax.axis_index("seq")
        self.x = lax.axis_index("mp")
        self.z = lax.div(seq, NY * 2)
        self.y = lax.rem(lax.div(seq, 2), NY)
        self.c = lax.rem(seq, 2)
        self.o = 1 - self.c
        self.yw = self.y + 1 - 2 * lax.rem(self.y, 2)
        z, y, c, x = self.z, self.y, self.c, self.x
        self.sib = self.at(z, y, self.o, x)
        self.zp, self.zm = self.at(mod(z + 1, NZ), y, c, x), self.at(mod(z - 1, NZ), y, c, x)
        self.yp, self.ym = self.at(z, mod(y + 1, NY), c, x), self.at(z, mod(y - 1, NY), c, x)
        self.xp, self.xm = (self.at(z, y, c, mod(x + 1, NX)), self.at(z, y, c, mod(x - 1, NX)))
        self.xo = self.at(z, y, c, mod(x + 2, NX))
        self.mate = self.at(z, self.yw, c, x)
        self.diag = self.at(z, self.yw, self.o, x)
        self.w = lax.rem(y, 2) * 2 + c
        self.window = (
            (self.sib, lax.rem(y, 2) * 2 + self.o),
            (self.mate, lax.rem(self.yw, 2) * 2 + c),
            (self.diag, lax.rem(self.yw, 2) * 2 + self.o),
        )

    def at(self, z, y, c, x):
        return ((z * NY + y) * 2 + c, x)

    def enter(self):
        barrier = pltpu.get_barrier_semaphore()
        partners = (self.sib, self.diag, self.zp, self.zm, self.yp, self.ym, self.xp, self.xm, self.xo)
        for partner in partners:
            pl.semaphore_signal(barrier, inc=1, device_id=partner, device_id_type=MESH)
        pl.semaphore_wait(barrier, len(partners))

    def send(self, src, dst, device):
        copy = pltpu.make_async_remote_copy(
            src_ref=src,
            dst_ref=dst,
            send_sem=self.send_sem.at[self.used],
            recv_sem=self.recv_sem.at[self.used],
            device_id=device,
            device_id_type=MESH,
        )
        self.used += 1
        self.sent.append(copy)
        copy.start()
        return copy

    def finish(self):
        for copy in self.sent:
            copy.wait_send()


def arrive(*copies):
    for copy in copies:
        copy.wait_recv()


class MpSum:
    def __init__(self, net, part, first, second):
        self.net, self.part, self.first, self.second = net, part, first, second

    def a(self):
        net, far = self.net, mod(self.net.x + 2, NX)
        self.copies = (
            net.send(self.part.at[far, 0], self.first.at[0], net.xp),
            net.send(self.part.at[far, 1], self.first.at[1], net.xm),
        )

    def b(self):
        net = self.net
        right, left = mod(net.x + 1, NX), mod(net.x - 1, NX)
        arrive(*self.copies)
        self.part[right, 0] = (self.part[right, 0].astype(F32) + self.first[0].astype(F32)).astype(BF16)
        self.part[left, 1] = (self.part[left, 1].astype(F32) + self.first[1].astype(F32)).astype(BF16)
        self.copies = (
            net.send(self.part.at[right], self.second.at[0], net.xp),
            net.send(self.part.at[left], self.second.at[1], net.xm),
        )

    def c(self):
        arrive(*self.copies)
        return self.part[self.net.x].astype(F32) + self.second[0].astype(F32) + self.second[1].astype(F32)


class MpGather:
    def __init__(self, net, full, lanes):
        self.net, self.full, self.lanes = net, full, lanes

    def a(self):
        net, block = self.net, self.full.at[self.net.x, :, self.lanes]
        self.copies = (net.send(block, block, net.xp), net.send(block, block, net.xm))

    def b(self):
        net = self.net
        arrive(*self.copies)
        left = self.full.at[mod(net.x - 1, NX), 0 : BLK // 2, self.lanes]
        right = self.full.at[mod(net.x + 1, NX), BLK // 2 : BLK, self.lanes]
        self.copies = (net.send(left, left, net.xp), net.send(right, right, net.xm))

    def c(self):
        arrive(*self.copies)


def chain(net, n, pos, right, left, block, from_left, from_right):
    hops = n // 2
    half = HALF // 2
    far = mod(pos + hops, n)
    low = net.send(block(far, 0, half), from_left.at[0, ..., 0:half], right)
    high = net.send(block(far, half, HALF), from_right.at[0, ..., half:HALF], left)
    yield
    for step in range(1, hops):
        lo, hi = (0, half) if step == 1 else (0, HALF)
        target = block(mod(pos + hops - step, n), lo, hi)
        arrive(low)
        target[...] = (target[...].astype(F32) + from_left[step - 1, ..., lo:hi].astype(F32)).astype(BF16)
        low = net.send(block(mod(pos + hops - step, n), 0, HALF), from_left.at[step], right)
        lo, hi = (half, HALF) if step == 1 else (0, HALF)
        target = block(mod(pos - hops + step, n), lo, hi)
        arrive(high)
        target[...] = (target[...].astype(F32) + from_right[step - 1, ..., lo:hi].astype(F32)).astype(BF16)
        high = net.send(block(mod(pos - hops + step, n), 0, HALF), from_right.at[step], left)
        yield
    arrive(low, high)


def seq_sum_parts(net, bufs, out):
    part, _, qa, qb, azl, azr, ayl, ayr, byl, byr, bzl, bzr = bufs
    z, y, c = net.z, net.y, net.c

    def half_a():
        block = lambda t, lo, hi: part.at[c, t, :, :, lo:hi]
        yield from chain(net, NZ, z, net.zp, net.zm, block, azl, azr)
        qa[...] = (
            part[c, z, :, :, 0:HALF].astype(F32) + azl[NZ // 2 - 1].astype(F32) + azr[NZ // 2 - 1].astype(F32)
        ).astype(BF16)
        block = lambda t, lo, hi: qa.at[t, :, lo:hi]
        yield from chain(net, NY, y, net.yp, net.ym, block, ayl, ayr)
        out[:, 0:HALF] = qa[y].astype(F32) + ayl[NY // 2 - 1].astype(F32) + ayr[NY // 2 - 1].astype(F32)

    def half_b():
        block = lambda t, lo, hi: part.at[c, :, t, :, HALF + lo : HALF + hi]
        yield from chain(net, NY, y, net.yp, net.ym, block, byl, byr)
        qb[...] = (
            part[c, :, y, :, HALF:QD].astype(F32) + byl[NY // 2 - 1].astype(F32) + byr[NY // 2 - 1].astype(F32)
        ).astype(BF16)
        block = lambda t, lo, hi: qb.at[t, :, lo:hi]
        yield from chain(net, NZ, z, net.zp, net.zm, block, bzl, bzr)
        out[:, HALF:QD] = qb[z].astype(F32) + bzl[NZ // 2 - 1].astype(F32) + bzr[NZ // 2 - 1].astype(F32)

    return [half_b(), half_a()]


def turn(parts):
    left = []
    for part in parts:
        try:
            next(part)
            left.append(part)
        except StopIteration:
            pass
    return left


def sum_cores(net, bufs, product):
    part, other = bufs[0], bufs[1]
    copies = []
    for pair in range(NZ // 2):
        rows = product(pair)
        for owner in range(NX):
            for place in range(2):
                z = 2 * pair + place
                y = (owner - z) % NY
                for core in range(2):
                    at = ((owner * 2 + place) * 2 + core) * CAP
                    part[core, z, y] = rows[at : at + CAP].astype(BF16)
        copies.append(
            net.send(part.at[net.o, 2 * pair : 2 * pair + 2], other.at[2 * pair : 2 * pair + 2], net.sib)
        )
    for pair in range(NZ // 2):
        arrive(copies[pair])
        for z in (2 * pair, 2 * pair + 1):
            part[net.c, z] = (part[net.c, z].astype(F32) + other[z].astype(F32)).astype(BF16)


def kernel(
    count_ref, onehot_ref, res_ref, cot_ref, rw_ref, win_ref, wout_ref,
    output_ref, grad_ref,
    send_sem, recv_sem, winp, woutp, counts, contrib, routed, g0, g1,
    pr, pra, prb, pd, pda, pdb, proj, dj, kv, joined, dproj, kg, kga, kgb,
    delta, dnormed, stats, fin, *chains,
):
    net = Net(send_sem, recv_sem)
    x, y, z, c = net.x, net.y, net.z, net.c
    net.enter()

    counts[net.w] = count_ref[...]
    copies = [net.send(count_ref, counts.at[net.w], partner) for partner, _ in net.window]
    winp[:, 768:896] = jnp.zeros((QD, 128), BF16)
    winp[:, 0:WIN] = win_ref[...]
    woutp[0:WOUT] = wout_ref[...]
    woutp[WOUT:WOUTP] = jnp.zeros((WOUTP - WOUT, QD), BF16)
    arrive(*copies)
    before = jnp.zeros((1, 128), jnp.int32)
    for place in range(4):
        earlier = jnp.where(place < net.w, jnp.int32(1), jnp.int32(0))
        before = before + counts[place, 0:1, :] * earlier
    at_row = lax.broadcasted_iota(jnp.int32, (64, 128), 0)
    at_slot = lax.broadcasted_iota(jnp.int32, (64, 128), 1)
    place_of = jnp.where(at_row - at_slot == before, F32(1.0), F32(0.0)).astype(BF16)
    sel = dot_nn(place_of, onehot_ref[...]).astype(BF16)

    copies = []
    for which, source in enumerate((res_ref, cot_ref)):
        contrib[which] = dot_nn(sel, source[...]).astype(BF16).reshape(4, CAP, QD)
        copies.append(
            [
                net.send(contrib.at[which, theirs], routed.at[which, slot], partner)
                for slot, (partner, theirs) in enumerate(net.window)
            ]
        )
    for which, g in enumerate((g0, g1)):
        arrive(*copies[which])
        total = contrib[which, net.w].astype(F32)
        for slot in range(3):
            total = total + routed[which, slot].astype(F32)
        g[z, y, c] = total.astype(BF16)

    def same(ref, device):
        return net.send(ref, ref, device)

    own = g0.at[z, y, c]
    r_copies = (same(own, net.yp), same(own, net.ym))
    own = g1.at[z, y, c]
    d_copies = (same(own, net.zp), same(own, net.zm))
    arrive(*r_copies)
    r_copies = (
        same(g0.at[z, mod(y - 1, NY), c, :, 0:HALF], net.yp),
        same(g0.at[z, mod(y + 1, NY), c, :, HALF:QD], net.ym),
    )

    def d_ring(step):
        arrive(*d_copies)
        if step < 4:
            return (
                same(g1.at[mod(z - step + 1, NZ), y, c], net.zp),
                same(g1.at[mod(z + step - 1, NZ), y, c], net.zm),
            )
        return (
            same(g1.at[mod(z - 3, NZ), y, c, :, 0:HALF], net.zp),
            same(g1.at[mod(z + 3, NZ), y, c, :, HALF:QD], net.zm),
        )

    d_copies = d_ring(2)
    arrive(*r_copies)
    r_copies = (same(g0.at[z, :, c], net.zp), same(g0.at[z, :, c], net.zm))
    sib_own = same(g0.at[z, :, c], net.sib)
    d_copies = d_ring(3)
    d_copies = d_ring(4)

    lane = lax.broadcasted_iota(jnp.int32, (BLK, 128), 1)

    def in_stage(stage, pair):
        rows = g0[pl.ds(2 * pair, 2)].reshape(BLK, QD)
        result = dot_nn(rows, winp[...])
        rows_f = rows.astype(F32)
        tail = result[:, 768:896]
        at = WIN - 768
        for value in (
            jnp.sum(rows_f * rows_f, axis=-1, keepdims=True),
            jnp.sum(rows_f * rw_ref[...], axis=-1, keepdims=True),
        ):
            for _ in range(3):
                rounded = value.astype(BF16).astype(F32)
                tail = jnp.where(lane == at, rounded, tail)
                value = value - rounded
                at += 1
        result = result.astype(BF16)
        tail = tail.astype(BF16)
        for place in range(2):
            for row in range(NY):
                owner = lax.rem(2 * pair + place + row, NX)
                at = (place * NY + row) * 32
                pr[stage, owner, place, :, 0:768] = result[at : at + 32, 0:768]
                pr[stage, owner, place, :, 768:896] = tail[at : at + 32]
        summed = MpSum(net, pr.at[stage], pra.at[stage], prb.at[stage])
        summed.a()
        return summed, pair

    def in_done(item):
        summed, pair = item
        proj[pl.ds(2 * pair, 2)] = summed.c()

    def back_stage(stage, row):
        rows = g1[:, row].reshape(BLK, QD)
        result = dot_nt(rows, woutp[...]).astype(BF16)
        for place in range(NZ):
            owner = lax.rem(row + place, NX)
            pd[stage, owner, place // 4] = result[place * 32 : place * 32 + 32]
        summed = MpSum(net, pd.at[stage], pda.at[stage], pdb.at[stage])
        summed.a()
        return summed, row

    def back_done(item):
        summed, row = item
        total = summed.c()
        first = mod(x - row, NX)
        dj[first] = total[0]
        dj[first + 4] = total[1]

    pair = lax.div(z, 2)
    turned = 2 * lax.rem(z, 2) - 1
    order = (pair, mod(pair + turned, 4), mod(pair - turned, 4), mod(pair + 2, 4))

    def r_ring(step):
        arrive(*r_copies)
        if step < 4:
            near, far = mod(z - step + 1, NZ), mod(z + step - 1, NZ)
            copies = (same(g0.at[near, :, c], net.zp), same(g0.at[far, :, c], net.zm))
        else:
            near, far = mod(z - 3, NZ), mod(z + 3, NZ)
            copies = (
                same(g0.at[near, :, c, :, 0:HALF], net.zp),
                same(g0.at[far, :, c, :, HALF:QD], net.zm),
            )
        return copies, (same(g0.at[near, :, c], net.sib), same(g0.at[far, :, c], net.sib))

    r_copies, sibs = r_ring(2)
    arrive(*d_copies)
    d_copies = (same(g1.at[:, y, c], net.yp), same(g1.at[:, y, c], net.ym))
    d_sib = same(g1.at[:, y, c], net.sib)
    arrive(sib_own, *sibs)
    in_1 = in_stage(0, order[0])
    r_copies, sibs = r_ring(3)
    arrive(d_sib)
    back_1 = back_stage(0, y)
    in_1[0].b()
    arrive(*sibs)
    in_2 = in_stage(1, order[1])
    r_copies, sibs = r_ring(4)
    back_1[0].b()
    in_2[0].b()
    arrive(*d_copies)
    below, above = mod(y - 1, NY), mod(y + 1, NY)
    d_copies = (
        same(g1.at[:, below, c, :, 0:HALF], net.yp),
        same(g1.at[:, above, c, :, HALF:QD], net.ym),
    )
    d_sibs = (same(g1.at[:, below, c], net.sib), same(g1.at[:, above, c], net.sib))
    arrive(*sibs)
    in_3 = in_stage(2, order[2])
    arrive(*r_copies)
    sib_last = same(g0.at[mod(z + 4, NZ), :, c], net.sib)
    arrive(d_sibs[0])
    back_2 = back_stage(1, below)
    in_3[0].b()
    arrive(sib_last)
    in_4 = in_stage(3, order[3])
    back_2[0].b()
    arrive(d_sibs[1])
    back_3 = back_stage(2, above)
    in_4[0].b()
    arrive(*d_copies)
    opposite = mod(y + 2, NY)
    d_last = same(g1.at[:, opposite, c], net.sib)
    back_3[0].b()
    in_done(in_1)
    in_done(in_2)
    arrive(d_last)
    back_4 = back_stage(3, opposite)
    in_done(in_3)
    in_done(in_4)
    back_4[0].b()

    tail = proj[:, :, 768:896].reshape(BLK, 128)
    at = WIN - 768
    square = jnp.sum(jnp.where((lane >= at) & (lane < at + 3), tail, 0.0), axis=-1, keepdims=True)
    logit = jnp.sum(jnp.where((lane >= at + 3) & (lane < at + 6), tail, 0.0), axis=-1, keepdims=True)
    in_scale = lax.rsqrt(square / D + 1e-05)
    gate = jax.nn.sigmoid(logit)
    query = proj[:, :, 0:HS].reshape(BLK, HS) * in_scale
    keyraw = proj[:, :, HS : 2 * HS].reshape(BLK, HS) * in_scale
    values = proj[:, :, 2 * HS : 3 * HS].reshape(BLK, HS) * in_scale
    query_scale = lax.rsqrt(jnp.mean(query * query, axis=-1, keepdims=True) + 1e-06)
    key_scale = lax.rsqrt(jnp.mean(keyraw * keyraw, axis=-1, keepdims=True) + 1e-06)
    query_b = (query * query_scale).astype(BF16)
    kv[x, :, 0:HS] = (keyraw * key_scale).astype(BF16)
    kv[x, :, HS : 2 * HS] = values.astype(BF16)
    kv_ring = MpGather(net, kv, slice(0, 2 * HS))
    kv_ring.a()

    gate_up = proj[:, :, 384:896].reshape(BLK, 512) * in_scale
    gate_in = gate_up[:, 0:FFD]
    up_in = gate_up[:, FFD : 2 * FFD]
    sigma = jax.nn.sigmoid(gate_in)
    joined[x, :, 256:384] = jnp.zeros((BLK, 128), BF16)
    joined[x, :, HS : HS + FFD] = (gate_in * sigma * up_in).astype(BF16)
    hid_ring = MpGather(net, joined, slice(HS, WOUTP))
    hid_ring.a()

    for item in (back_1, back_2, back_3, back_4):
        back_done(item)
    dattended = (dj[:, :, 0:HS].reshape(BLK, HS) * gate).astype(BF16)
    dhidden = dj[:, :, HS:WOUTP].reshape(BLK, 256)[:, 0:FFD] * gate
    dup = (dhidden * gate_in * sigma).astype(BF16)
    dgate_in = (dhidden * up_in * sigma * (1.0 + gate_in * (1.0 - sigma))).astype(BF16)
    dproj[x, :, 384:896] = jnp.concatenate([dgate_in, dup, jnp.zeros((BLK, 64), BF16)], axis=-1)
    ff_ring = MpGather(net, dproj, slice(384, WINP))
    kv_ring.b()
    ff_ring.a()
    hid_ring.b()
    kv_ring.c()

    keys = kv[:, :, 0:HS].reshape(ROWS, HS)
    vals = kv[:, :, HS : 2 * HS].reshape(ROWS, HS)
    row = lax.broadcasted_iota(jnp.int32, (BLK, 1), 0)
    row_z = row >> 5
    query_order = row_z * 128 + ((x + 8 - row_z) & 3) * 32 + (row & 31)
    col = lax.broadcasted_iota(jnp.int32, (1, ROWS), 1)
    col_z = (col >> 5) & 7
    key_order = col_z * 128 + (((col >> 8) + 8 - col_z) & 3) * 32 + (col & 31)
    visible = key_order <= query_order
    expo = jnp.where(visible, jnp.exp(dot_nt(query_b, keys) * FACTOR), 0.0)
    inverse = 1.0 / jnp.sum(expo, axis=-1, keepdims=True)
    joined[x, :, 0:HS] = (dot_nn(expo.astype(BF16), vals) * inverse).astype(BF16)
    att_ring = MpGather(net, joined, slice(0, HS))
    att_ring.a()

    prob = expo * inverse
    dprob = dot_nt(dattended, vals)
    inner = jnp.sum(prob * dprob, axis=-1, keepdims=True)
    dscore = (prob * (dprob - inner)).astype(BF16)
    prob_b = prob.astype(BF16)
    dkey_part = dot_tn(dscore, query_b) * FACTOR
    dvalue_part = dot_tn(prob_b, dattended)
    for owner in range(NX):
        for place in range(2):
            at = (owner * 2 + place) * 128
            kg[owner, place, :, 0:HS] = dkey_part[at : at + 128].astype(BF16)
            kg[owner, place, :, HS : 2 * HS] = dvalue_part[at : at + 128].astype(BF16)
    kg_sum = MpSum(net, kg, kga, kgb)
    kg_sum.a()
    att_ring.b()
    dquery_n = dot_nn(dscore, keys) * FACTOR
    ff_ring.b()

    def norm_back(values, scale, grads):
        return scale * grads - values * scale**3 * jnp.mean(grads * values, axis=-1, keepdims=True)

    dproj[x, :, 0:HS] = norm_back(query, query_scale, dquery_n).astype(BF16)
    kg_sum.b()
    hid_ring.c()
    att_ring.c()

    delta_bufs, dnormed_bufs = chains[:12], chains[12:]

    def delta_rows(pair):
        return dot_nn(joined[:, pair * 64 : pair * 64 + 64].reshape(BLK, WOUTP), woutp[...])

    sum_cores(net, delta_bufs, delta_rows)
    parts = turn(seq_sum_parts(net, delta_bufs, delta))
    key_grad = kg_sum.c().reshape(BLK, 2 * HS)
    dproj[x, :, HS : 2 * HS] = norm_back(keyraw, key_scale, key_grad[:, 0:HS]).astype(BF16)
    dproj[x, :, 2 * HS : 3 * HS] = key_grad[:, HS : 2 * HS].astype(BF16)
    qkv_ring = MpGather(net, dproj, slice(0, 3 * HS))
    qkv_ring.a()
    parts = turn(parts)
    qkv_ring.b()
    parts = turn(parts)
    ff_ring.c()
    qkv_ring.c()

    def dnormed_rows(pair):
        return dot_nt(dproj[:, pair * 64 : pair * 64 + 64].reshape(BLK, WINP), winp[...])

    sum_cores(net, dnormed_bufs, dnormed_rows)
    more = turn(seq_sum_parts(net, dnormed_bufs, dnormed))
    while parts or more:
        parts = turn(parts)
        more = turn(more)

    rows = g0[z, y, c].astype(F32)
    grads = g1[z, y, c].astype(F32)
    rw = rw_ref[...]
    delta_b = delta[...].astype(BF16).astype(F32)
    dn = dnormed[...]
    small = lax.broadcasted_iota(jnp.int32, (CAP, 128), 1)
    tile = jnp.zeros((CAP, 128), F32)
    for at, product in enumerate((rows * rows, rows * rw, grads * delta_b, dn * rows)):
        tile = jnp.where(small == at, jnp.sum(product, axis=-1, keepdims=True), tile)
    stats[3] = tile
    arrive(*[net.send(stats.at[3], stats.at[slot], device) for slot, device in enumerate((net.xp, net.xo, net.xm))])
    tile = stats[0] + stats[1] + stats[2] + stats[3]

    def pick(at):
        return jnp.sum(jnp.where(small == at, tile, 0.0), axis=-1, keepdims=True)

    in_scale = lax.rsqrt(pick(0) / D + 1e-05)
    gate = jax.nn.sigmoid(pick(1))
    dlogit = pick(2) * gate * (1.0 - gate)
    dinput = (in_scale * dn - rows * in_scale**3 * (pick(3) / D)).astype(BF16).astype(F32)
    fin[0, net.w] = (rows + gate * delta_b).astype(BF16)
    fin[1, net.w] = (grads + dinput + dlogit * rw).astype(BF16)
    copies = [
        net.send(fin.at[which, net.w], fin.at[which, net.w], partner)
        for which in range(2)
        for partner, _ in net.window
    ]
    chosen = dot_tn(sel, jnp.ones((64, 128), BF16))[:, 0:1] > 0.5
    for which, (source, target) in enumerate(((res_ref, output_ref), (cot_ref, grad_ref))):
        arrive(*copies[which * 3 : which * 3 + 3])
        back = dot_tn(sel, fin[which].reshape(64, QD)).astype(BF16)
        target[...] = jnp.where(chosen, back, source[...])
    net.finish()


def chain_scratch():
    return [
        pltpu.VMEM((2, NZ, NY, CAP, QD), BF16),
        pltpu.VMEM((NZ, NY, CAP, QD), BF16),
        pltpu.VMEM((NY, CAP, HALF), BF16),
        pltpu.VMEM((NZ, CAP, HALF), BF16),
        pltpu.VMEM((NZ // 2, NY, CAP, HALF), BF16),
        pltpu.VMEM((NZ // 2, NY, CAP, HALF), BF16),
        pltpu.VMEM((NY // 2, CAP, HALF), BF16),
        pltpu.VMEM((NY // 2, CAP, HALF), BF16),
        pltpu.VMEM((NY // 2, NZ, CAP, HALF), BF16),
        pltpu.VMEM((NY // 2, NZ, CAP, HALF), BF16),
        pltpu.VMEM((NZ // 2, CAP, HALF), BF16),
        pltpu.VMEM((NZ // 2, CAP, HALF), BF16),
    ]


def local(residual, chosen_pos, chosen_count, router_weight, weight_in, weight_out, cotangent):
    slots = jnp.arange(128, dtype=jnp.int32)
    position = jnp.pad(chosen_pos, (0, 128 - chosen_pos.shape[0]))
    onehot = ((position[:, None] == slots[None, :]) & (slots < chosen_count[0])[:, None]).astype(BF16)
    counts = jnp.broadcast_to(chosen_count[0], (8, 128)).astype(jnp.int32)
    n_sem = 192
    scratch = [
        pltpu.SemaphoreType.DMA((n_sem,)),
        pltpu.SemaphoreType.DMA((n_sem,)),
        pltpu.VMEM((QD, WINP), BF16),
        pltpu.VMEM((WOUTP, QD), BF16),
        pltpu.VMEM((4, 8, 128), jnp.int32),
        pltpu.VMEM((2, 4, CAP, QD), BF16),
        pltpu.VMEM((2, 3, CAP, QD), BF16),
        pltpu.VMEM((NZ, NY, 2, CAP, QD), BF16),
        pltpu.VMEM((NZ, NY, 2, CAP, QD), BF16),
        pltpu.VMEM((4, NX, 2, 32, WINP), BF16),
        pltpu.VMEM((4, 2, 32, WINP), BF16),
        pltpu.VMEM((4, 2, 2, 32, WINP), BF16),
        pltpu.VMEM((4, NX, 2, 32, WOUTP), BF16),
        pltpu.VMEM((4, 2, 32, WOUTP), BF16),
        pltpu.VMEM((4, 2, 2, 32, WOUTP), BF16),
        pltpu.VMEM((NZ, 32, WINP), F32),
        pltpu.VMEM((NZ, 32, WOUTP), F32),
        pltpu.VMEM((NX, BLK, 2 * HS), BF16),
        pltpu.VMEM((NX, BLK, WOUTP), BF16),
        pltpu.VMEM((NX, BLK, WINP), BF16),
        pltpu.VMEM((NX, 2, 128, 2 * HS), BF16),
        pltpu.VMEM((2, 128, 2 * HS), BF16),
        pltpu.VMEM((2, 2, 128, 2 * HS), BF16),
        pltpu.VMEM((CAP, QD), F32),
        pltpu.VMEM((CAP, QD), F32),
        pltpu.VMEM((4, CAP, 128), F32),
        pltpu.VMEM((2, 4, CAP, QD), BF16),
    ] + chain_scratch() + chain_scratch()
    vmem = pl.BlockSpec(memory_space=pltpu.VMEM)
    return pl.pallas_call(
        kernel,
        out_shape=[jax.ShapeDtypeStruct(residual.shape, BF16)] * 2,
        in_specs=[vmem] * 7,
        out_specs=[vmem] * 2,
        scratch_shapes=scratch,
        compiler_params=pltpu.CompilerParams(
            collective_id=0, has_side_effects=True, vmem_limit_bytes=62 * 1024 * 1024
        ),
        cost_estimate=pl.CostEstimate(flops=10**10, bytes_accessed=10**7, transcendentals=10**6),
    )(counts, onehot, residual, cotangent, router_weight[None, :], weight_in, weight_out)


def solution(mesh):
    spec = P("seq", "mp")
    return jax.shard_map(
        local,
        mesh=mesh,
        in_specs=(spec, P("seq"), P("seq"), P("mp"), P("mp", "seq"), spec, spec),
        out_specs=(spec, spec),
        check_vma=False,
    )
```

time: 865 us -> 177 us (0.20)
  waiting for transfers between devices: 641 us -> 0 us
  Pallas kernels: 0 us -> 163 us
  blocking collectives: 58.6 us -> 0 us
  starting transfers between devices: 56.1 us -> 0 us
  matrix products: 48 us -> 0 us
  other arithmetic: 19 us -> 0.72 us
  between operations: 15.4 us -> 1.29 us
  local copies, waits for them, and re-layouts: 21.7 us -> 11.1 us
    reduce_scatter x5 -> x0, waiting for transfers between devices: 364 us -> none  [the longest x1 150 us: local(): lax.psum_scatter(jnp.dot(piece, weight_out, preferred_element_type=jnp.fl...]
    all_gather x3 -> x0, waiting for transfers between devices: 266 us -> none  [the longest x2 232 us: gather_rows(): return lax.all_gather(block, 'seq', axis=0, tiled=True)]
    pallas_call x0 -> x1, Pallas kernels: none -> 163 us  [local(): pl.pallas_call(kernel, out_shape=[jax.ShapeDtypeStruct(residual.shape, BF...]
    ppermute x16 -> x0, starting transfers between devices: 55.6 us -> none  [shifted(): lax.ppermute(value, axis, [(source, source + steps) for source in range(f...]
    dot_general x30 -> x0, matrix products: 48 us -> none  [the longest x10 9.4 us: route_in(): jnp.dot(selector, row_block, preferred_element_type=jnp.float32)]
    all_gather x2 -> x0, blocking collectives: 20.9 us -> none  [the longest x1 10.9 us: local(): joined_all = lax.all_gather(joined, 'mp', axis=0, tiled=True)]
    unnamed x1 -> x0, blocking collectives: 20.7 us -> none
    psum x2 -> x0, blocking collectives: 17 us -> none  [the longest x1 8.57 us: local(): square_sum = lax.psum(jnp.sum(own_rows * own_rows, axis=-1), 'mp')]
  transfers between devices with their start and end apart: 24 -> 0, of which waited for: 14 -> 0; matrix products, arithmetic and copies ran while one was open for 2% -> 0% of each run, Pallas kernels for 0% -> 0%
where the time goes in v1:
time: 177 us
  Pallas kernels  163 us (92%)
  local copies, waits for them, and re-layouts  11.1 us (6%)
    pallas_call x1, Pallas kernels, local(): pl.pallas_call(kernel, out_shape=[jax.ShapeDtypeStruct(residual.shape, BF...  163 us
    unnamed x3, local copies, waits for them, and re-layouts  9.8 us

profile of v1, /device:TPU:1, one launch (start us, length us, event | category | flops | bytes accessed | tf_op | source)
XLA Modules:
  0.0 176.5 jit_solution(1100287556783950322)
XLA Ops:
  1.3 0.7 pad.4
  1.9 0.6 broadcast_in_dim.4.count_ref
  2.5 0.7 fusion.1.onehot_ref
  3.3 6.0 %copy.9.win_ref = bf16[2048,832]{1,0:T(8,128)(2,1)} copy(bf16[2048,832]{0,1:T(8,128)(2,1)} %param.11) | data formatting | bytes 6815744 | tf_op args[4]
  9.3 163.5 %shard_map.86 = (bf16[128,2048]{1,0:T(8,128)(2,1)}, bf16[128,2048]{1,0:T(8,128)(2,1)}) custom-call(s32[8,128]{1,0:T(8,128)} %broadcast_in_dim.4.count_ref, bf16[128,128]{1,0:T(8,128)(2,1)} %fusion.1.onehot_ref, bf16[128,2048]{1,0:T(8,128)(2,1)} %res_ref.1, bf16[128,2048]{1,0:T(8,128)(2,1)} %cot_ref.1, f32[1,2048]{1,0:T(1,128)} %bitcast.4, ...), custom_call_target="tpu_custom_call" | custom-call | flops 10000000000 | bytes 10000000 | tf_op jit(solution)/shard_map/pallas_call | solution.py:617
  172.7 1.9 %copy.13 = bf16[128,2048]{1,0:T(8,128)(2,1)} copy(bf16[128,2048]{1,0:T(8,128)(2,1)} %get-tuple-element.4) | data formatting | bytes 1048576
  174.6 1.9 %copy.14 = bf16[128,2048]{1,0:T(8,128)(2,1)} copy(bf16[128,2048]{1,0:T(8,128)(2,1)} %get-tuple-element.5) | data formatting | bytes 1048576
  (1 shorter events, 0.0 us)

commit v2 on v1

v2 whole, which is shorter than its diff:
```python
import jax
import jax.numpy as jnp
from jax import lax
from jax.experimental import pallas as pl
from jax.experimental.pallas import tpu as pltpu
from jax.sharding import PartitionSpec as P

MESH = pl.DeviceIdType.MESH
D = 8192
HS = 128
NZ, NY, NX = 8, 4, 4
CAP = 16
QD = D // NX
FFD = 224
WIN = 3 * HS + 2 * FFD
WINP = 896
WOUT = HS + FFD
WOUTP = 384
PRW = WINP + WOUTP
ROWS = 1024
BLK = 256
HALF = QD // 2
F32 = jnp.float32
BF16 = jnp.bfloat16
FACTOR = HS ** (-0.5)


def mod(value, n):
    return lax.rem(value + n, n)


def dot_nn(a, b):
    return jnp.dot(a, b, preferred_element_type=F32)


def dot_nt(a, b):
    return lax.dot_general(a, b, (((1,), (1,)), ((), ())), preferred_element_type=F32)


def dot_tn(a, b):
    return lax.dot_general(a, b, (((0,), (0,)), ((), ())), preferred_element_type=F32)


class Net:
    def __init__(self, send_sem, recv_sem):
        self.send_sem, self.recv_sem = send_sem, recv_sem
        self.used = 0
        self.sent = []
        seq = lax.axis_index("seq")
        x = self.x = lax.axis_index("mp")
        z = self.z = lax.div(seq, NY * 2)
        y = self.y = lax.rem(lax.div(seq, 2), NY)
        c = self.c = lax.rem(seq, 2)
        self.o = 1 - c
        self.upper = lax.rem(y, 2)
        self.w = self.upper * 2 + c
        yw = y + 1 - 2 * self.upper
        yo = mod(y - 1 + 2 * self.upper, NY)
        self.twin = self.at(z, y, self.o, x)
        self.mate = self.at(z, yw, c, x)
        self.cross = self.at(z, yw, self.o, x)
        self.beyond = self.at(z, yo, c, x)
        self.along_x = [self.at(z, y, c, mod(x + d, NX)) for d in range(1, NX)]
        self.along_y = [self.at(z, mod(y + d, NY), c, x) for d in range(1, NY)]
        self.along_z = [self.at(mod(z + d, NZ), y, c, x) for d in range(1, NZ)]
        self.xp, self.xm = self.along_x[0], self.along_x[-1]
        self.yp, self.ym = self.along_y[0], self.along_y[-1]
        self.zp, self.zm = self.along_z[0], self.along_z[-1]

    def at(self, z, y, c, x):
        return ((z * NY + y) * 2 + c, x)

    def enter(self):
        barrier = pltpu.get_barrier_semaphore()
        partners = [self.twin, self.cross] + self.along_x + self.along_y + self.along_z
        for partner in partners:
            pl.semaphore_signal(barrier, inc=1, device_id=partner, device_id_type=MESH)
        pl.semaphore_wait(barrier, len(partners))

    def send(self, src, dst, device):
        copy = pltpu.make_async_remote_copy(
            src_ref=src,
            dst_ref=dst,
            send_sem=self.send_sem.at[self.used],
            recv_sem=self.recv_sem.at[self.used],
            device_id=device,
            device_id_type=MESH,
        )
        self.used += 1
        self.sent.append(copy)
        copy.start()
        return copy

    def same(self, ref, device):
        return self.send(ref, ref, device)

    def finish(self):
        for copy in self.sent:
            copy.wait_send()


def arrive(*copies):
    for copy in copies:
        copy.wait_recv()


class MpSum:
    def __init__(self, net, part, landed):
        self.net, self.part, self.landed = net, part, landed
        self.copies = [
            net.send(part.at[mod(net.x + d, NX)], landed.at[d - 1], net.along_x[d - 1]) for d in range(1, NX)
        ]

    def total(self):
        arrive(*self.copies)
        total = self.part[self.net.x].astype(F32)
        for d in range(NX - 1):
            total = total + self.landed[d].astype(F32)
        return total


class MpGather:
    def __init__(self, net, full, lanes):
        block = full.at[net.x, :, lanes]
        self.copies = [net.same(block, device) for device in net.along_x]

    def done(self):
        arrive(*self.copies)


class MpRing:
    def __init__(self, net, full, lanes):
        self.net, self.full, self.lanes = net, full, lanes
        block = full.at[net.x, :, lanes]
        self.copies = (net.same(block, net.xp), net.same(block, net.xm))

    def pass_on(self):
        net = self.net
        arrive(*self.copies)
        left = self.full.at[mod(net.x - 1, NX), 0 : BLK // 2, self.lanes]
        right = self.full.at[mod(net.x + 1, NX), BLK // 2 : BLK, self.lanes]
        self.copies = (net.same(left, net.xp), net.same(right, net.xm))

    def done(self):
        arrive(*self.copies)


def chain(net, pos, block, from_left, from_right, width):
    hops = NZ // 2
    half = width // 2
    far = mod(pos + hops, NZ)
    low = net.send(block(far, 0, half), from_left.at[0, ..., 0:half], net.zp)
    high = net.send(block(far, half, width), from_right.at[0, ..., half:width], net.zm)
    yield
    for step in range(1, hops):
        lo, hi = (0, half) if step == 1 else (0, width)
        target = block(mod(pos + hops - step, NZ), lo, hi)
        arrive(low)
        target[...] = (target[...].astype(F32) + from_left[step - 1, ..., lo:hi].astype(F32)).astype(BF16)
        low = net.send(block(mod(pos + hops - step, NZ), 0, width), from_left.at[step], net.zp)
        lo, hi = (half, width) if step == 1 else (0, width)
        target = block(mod(pos - hops + step, NZ), lo, hi)
        arrive(high)
        target[...] = (target[...].astype(F32) + from_right[step - 1, ..., lo:hi].astype(F32)).astype(BF16)
        high = net.send(block(mod(pos - hops + step, NZ), 0, width), from_right.at[step], net.zm)
        yield
    arrive(low, high)


class SeqSum:
    def __init__(self, net, bufs, out, product, order):
        self.net, self.bufs, self.out, self.product, self.order = net, bufs, out, product, order
        self.by_copies = []
        self.steps = [self.along_z_first(0), self.along_z_first(1)]

    def multiply(self):
        net, part, other = self.net, self.bufs[0], self.bufs[1]
        self.copies = []
        for k, pair in enumerate(self.order):
            rows = self.product(pair)
            for owner in range(NX):
                for place in range(2):
                    z = 2 * pair + place
                    y = lax.rem(owner - z + 2 * NZ, NY)
                    for core in range(2):
                        at = ((owner * 2 + place) * 2 + core) * CAP
                        part[core, z, y] = rows[at : at + CAP].astype(BF16)
            both = pl.ds(2 * pair, 2)
            self.copies.append(net.send(part.at[net.o, both], other.at[both], net.twin))
            if k:
                self.merge(k - 1)
        self.merge(len(self.order) - 1)
        self.steps.append(self.along_y_first())

    def merge(self, k):
        net, part, other, byl = self.net, self.bufs[0], self.bufs[1], self.bufs[7]
        arrive(self.copies[k])
        pair = self.order[k]
        for place in range(2):
            z = 2 * pair + place
            part[net.c, z] = (part[net.c, z].astype(F32) + other[z].astype(F32)).astype(BF16)
        if k == 0:
            for step in self.steps:
                next(step)
        both = pl.ds(2 * pair, 2)
        for d in range(1, NY):
            source = part.at[net.c, both, mod(net.y + d, NY), :, HALF:QD]
            self.by_copies.append(net.send(source, byl.at[d - 1, both], net.along_y[d - 1]))

    def turn(self):
        left = []
        for step in self.steps:
            try:
                next(step)
                left.append(step)
            except StopIteration:
                pass
        self.steps = left
        return bool(left)

    def along_z_first(self, which):
        net, part, qa, ayl = self.net, self.bufs[0], self.bufs[2], self.bufs[6]
        width = HALF // 2
        first = which * width
        left, right = self.bufs[4].at[which], self.bufs[5].at[which]
        block = lambda t, lo, hi: part.at[net.c, t, :, :, first + lo : first + hi]
        yield from chain(net, net.z, block, left, right, width)
        last = NZ // 2 - 1
        lanes = slice(first, first + width)
        qa[:, :, lanes] = (
            part[net.c, net.z, :, :, lanes].astype(F32) + left[last].astype(F32) + right[last].astype(F32)
        ).astype(BF16)
        copies = [
            net.send(qa.at[mod(net.y + d, NY), :, lanes], ayl.at[d - 1, :, lanes], net.along_y[d - 1])
            for d in range(1, NY)
        ]
        yield
        arrive(*copies)
        total = qa[net.y, :, lanes].astype(F32)
        for d in range(NY - 1):
            total = total + ayl[d, :, lanes].astype(F32)
        self.out[:, lanes] = total

    def along_y_first(self):
        net, part, qb, byl, bzl = self.net, self.bufs[0], self.bufs[3], self.bufs[7], self.bufs[8]
        arrive(*self.by_copies)
        total = part[net.c, :, net.y, :, HALF:QD].astype(F32)
        for d in range(NY - 1):
            total = total + byl[d].astype(F32)
        qb[...] = total.astype(BF16)
        copies = [net.send(qb.at[mod(net.z + d, NZ)], bzl.at[d - 1], net.along_z[d - 1]) for d in range(1, NZ)]
        yield
        arrive(*copies)
        total = qb[net.z].astype(F32)
        for d in range(NZ - 1):
            total = total + bzl[d].astype(F32)
        self.out[:, HALF:QD] = total


def row_sums(tile, columns):
    small = lax.broadcasted_iota(jnp.int32, tile, 1)
    result = jnp.zeros(tile, F32)
    for at, product in enumerate(columns):
        result = jnp.where(small == at, jnp.sum(product, axis=-1, keepdims=True), result)
    return result


def kernel(
    count_ref, pos_ref, res_ref, cot_ref, rw_ref, win_ref, wout_ref,
    fin_out, sel_out,
    send_sem, recv_sem, load_sem, winp, woutp, counts, contrib, from_twin, from_mate, g0, g1,
    pr, prl, proj, kv, joined, dproj, kg, kgl,
    delta, dnormed, stats, fin, *bufs,
):
    net = Net(send_sem, recv_sem)
    x, y, z, c = net.x, net.y, net.z, net.c
    loads = (
        pltpu.make_async_copy(win_ref, winp.at[0:WIN], load_sem.at[0]),
        pltpu.make_async_copy(wout_ref, woutp.at[0:WOUT], load_sem.at[1]),
    )
    for load in loads:
        load.start()
    net.enter()

    counts[0] = jnp.zeros((8, 128), jnp.int32) + count_ref[...]
    arrive(net.send(counts.at[0], counts.at[1], net.twin))
    n_slots = pos_ref.shape[1]
    mine, twins = counts[0, 0:1, 0:n_slots], counts[1, 0:1, 0:n_slots]
    before = twins * c + (4 * CAP - mine - twins) * net.upper
    row = lax.broadcasted_iota(jnp.int32, (4 * CAP, n_slots), 0)
    slot = lax.broadcasted_iota(jnp.int32, (4 * CAP, n_slots), 1)
    place_of = jnp.where(row - slot == before, F32(1.0), F32(0.0)).astype(BF16)
    token = lax.broadcasted_iota(jnp.int32, (128, n_slots), 0)
    slot = lax.broadcasted_iota(jnp.int32, (128, n_slots), 1)
    token_of = jnp.where((token == pos_ref[...]) & (slot < mine), F32(1.0), F32(0.0)).astype(BF16)
    sel = dot_nt(place_of, token_of).astype(BF16)
    sel_out[...] = sel

    copies = []
    for which, source in enumerate((res_ref, cot_ref)):
        rows = dot_nn(sel, source[...]).astype(BF16)
        for chip in range(2):
            for core in range(2):
                at = (chip * 2 + core) * CAP
                contrib[which, core, chip] = rows[at : at + CAP]
        copies.append(net.send(contrib.at[which, net.o], from_twin.at[which], net.twin))
    for which in range(2):
        arrive(copies[which])
        contrib[which, c] = (contrib[which, c].astype(F32) + from_twin[which].astype(F32)).astype(BF16)
        if which == 0:
            r_copy = net.send(contrib.at[0, c], from_mate.at[0:2], net.mate)
        else:
            d_copy = net.send(contrib.at[1, c, 1 - net.upper], from_mate.at[2], net.mate)
    mine_q = lax.div(y, 2)
    arrive(r_copy)
    for place in range(2):
        g0[z, 2 * mine_q + place, c] = (
            contrib[0, c, place].astype(F32) + from_mate[place].astype(F32)
        ).astype(BF16)

    def r_ring(step, q):
        near, far = mod(z - step + 1, NZ), mod(z + step - 1, NZ)
        ys = pl.ds(2 * q, 2)
        if step < 4:
            return (net.same(g0.at[near, ys, c], net.zp), net.same(g0.at[far, ys, c], net.zm))
        return (
            net.same(g0.at[near, ys, c, :, 0:HALF], net.zp),
            net.same(g0.at[far, ys, c, :, HALF:QD], net.zm),
        )

    def d_ring(step):
        near, far = mod(z - step + 1, NZ), mod(z + step - 1, NZ)
        if step < 4:
            return (net.same(g1.at[near, y, c], net.zp), net.same(g1.at[far, y, c], net.zm))
        return (
            net.same(g1.at[near, y, c, :, 0:HALF], net.zp),
            net.same(g1.at[far, y, c, :, HALF:QD], net.zm),
        )

    def d_sides(d):
        at = mod(z + d, NZ)
        return d, (net.same(g1.at[at, y, c], net.yp), net.same(g1.at[at, y, c], net.ym))

    def d_opposite(item):
        d, copies = item
        arrive(*copies)
        at = mod(z + d, NZ)
        return d, (
            net.same(g1.at[at, mod(y - 1, NY), c, :, 0:HALF], net.yp),
            net.same(g1.at[at, mod(y + 1, NY), c, :, HALF:QD], net.ym),
        )

    def d_twin(item):
        d, copies = item
        arrive(*copies)
        return net.same(g1.at[mod(z + d, NZ), :, c], net.twin)

    def r_twin(d):
        return net.same(g0.at[mod(z + d, NZ), :, c], net.twin)

    other_q = 1 - mine_q
    p_ring = r_ring(1, mine_q)
    r_copy = net.same(g0.at[z, pl.ds(2 * mine_q, 2), c], net.beyond)
    arrive(d_copy)
    g1[z, y, c] = (contrib[1, c, net.upper].astype(F32) + from_mate[2].astype(F32)).astype(BF16)
    g_ring = d_ring(1)
    d_0 = d_sides(0)
    rows = g0[z, y, c].astype(F32)
    stats[0, 3] = row_sums((CAP, 128), (rows * rows, rows * rw_ref[...]))
    first_stats = [net.send(stats.at[0, 3], stats.at[0, d], net.along_x[d]) for d in range(3)]
    winp[WIN:WINP] = jnp.zeros((WINP - WIN, QD), BF16)
    woutp[WOUT:WOUTP] = jnp.zeros((WOUTP - WOUT, QD), BF16)
    arrive(r_copy)
    q_ring = r_ring(1, other_q)
    r_0 = r_twin(0)
    arrive(*g_ring)
    g_ring = d_ring(2)
    d_1, d_7 = d_sides(1), d_sides(-1)
    d_0 = d_opposite(d_0)
    arrive(*p_ring)
    p_ring = r_ring(2, mine_q)
    arrive(*q_ring)
    q_ring = r_ring(2, other_q)
    r_1, r_7 = r_twin(1), r_twin(-1)
    arrive(*g_ring)
    g_ring = d_ring(3)
    d_2, d_6 = d_sides(2), d_sides(-2)
    d_0 = d_twin(d_0)
    d_1, d_7 = d_opposite(d_1), d_opposite(d_7)
    arrive(*p_ring)
    p_ring = r_ring(3, mine_q)
    arrive(*q_ring)
    q_ring = r_ring(3, other_q)
    r_2, r_6 = r_twin(2), r_twin(-2)
    d_1, d_7 = d_twin(d_1), d_twin(d_7)
    arrive(*g_ring)
    g_ring = d_ring(4)
    d_3, d_5 = d_sides(3), d_sides(-3)
    d_2, d_6 = d_opposite(d_2), d_opposite(d_6)

    lane = lax.broadcasted_iota(jnp.int32, (BLK, 128), 1)

    def stage(k, pair):
        both = pl.ds(2 * pair, 2)
        rows = g0[both].reshape(BLK, QD)
        result = dot_nt(rows, winp[...])
        rows_f = rows.astype(F32)
        tail = result[:, 768:896]
        at = WIN - 768
        for value in (
            jnp.sum(rows_f * rows_f, axis=-1, keepdims=True),
            jnp.sum(rows_f * rw_ref[...], axis=-1, keepdims=True),
        ):
            for _ in range(3):
                rounded = value.astype(BF16).astype(F32)
                tail = jnp.where(lane == at, rounded, tail)
                value = value - rounded
                at += 1
        result = result.astype(BF16)
        tail = tail.astype(BF16)
        back = dot_nt(g1[both].reshape(BLK, QD), woutp[...]).astype(BF16)
        for place in range(2):
            for row in range(NY):
                owner = lax.rem(2 * pair + place + row, NX)
                at = (place * NY + row) * 32
                pr[k, owner, place, :, 0:768] = result[at : at + 32, 0:768]
                pr[k, owner, place, :, 768:896] = tail[at : at + 32]
                pr[k, owner, place, :, WINP:PRW] = back[at : at + 32]
        return MpSum(net, pr.at[k], prl.at[k]), pair

    def stage_done(item):
        summed, pair = item
        proj[pl.ds(2 * pair, 2)] = summed.total()

    pair = lax.div(z, 2)
    turned = 2 * lax.rem(z, 2) - 1
    order = (pair, mod(pair + turned, 4), mod(pair - turned, 4), mod(pair + 2, 4))

    for load in loads:
        load.wait()
    arrive(r_0, r_1, r_7, d_0, d_1, d_7)
    s_0 = stage(0, order[0])
    arrive(*p_ring)
    p_ring = r_ring(4, mine_q)
    arrive(*q_ring)
    q_ring = r_ring(4, other_q)
    r_3, r_5 = r_twin(3), r_twin(-3)
    d_2, d_6 = d_twin(d_2), d_twin(d_6)
    arrive(*g_ring)
    d_4 = d_sides(4)
    d_3, d_5 = d_opposite(d_3), d_opposite(d_5)
    arrive(r_2, r_6, d_2, d_6)
    s_1 = stage(1, order[1])
    arrive(*p_ring)
    arrive(*q_ring)
    r_4 = r_twin(4)
    d_4 = d_opposite(d_4)
    d_3, d_5 = d_twin(d_3), d_twin(d_5)
    arrive(r_3, r_5, d_3, d_5)
    s_2 = stage(2, order[2])
    d_4 = d_twin(d_4)
    stage_done(s_0)
    arrive(r_4, d_4)
    s_3 = stage(3, order[3])
    stage_done(s_1)
    stage_done(s_2)
    stage_done(s_3)

    tail = proj[:, :, 768:896].reshape(BLK, 128)
    at = WIN - 768
    square = jnp.sum(jnp.where((lane >= at) & (lane < at + 3), tail, 0.0), axis=-1, keepdims=True)
    logit = jnp.sum(jnp.where((lane >= at + 3) & (lane < at + 6), tail, 0.0), axis=-1, keepdims=True)
    in_scale = lax.rsqrt(square / D + 1e-05)
    gate = jax.nn.sigmoid(logit)
    keyraw = proj[:, :, HS : 2 * HS].reshape(BLK, HS) * in_scale
    key_scale = lax.rsqrt(jnp.mean(keyraw * keyraw, axis=-1, keepdims=True) + 1e-06)
    kv[x, :, 0:HS] = (keyraw * key_scale).astype(BF16)
    kv[x, :, HS : 2 * HS] = (proj[:, :, 2 * HS : 3 * HS].reshape(BLK, HS) * in_scale).astype(BF16)
    kv_gather = MpGather(net, kv, slice(0, 2 * HS))

    gate_up = proj[:, :, 384:896].reshape(BLK, 512) * in_scale
    gate_in = gate_up[:, 0:FFD]
    up_in = gate_up[:, FFD : 2 * FFD]
    sigma = jax.nn.sigmoid(gate_in)
    joined[x, :, 256:384] = jnp.zeros((BLK, 128), BF16)
    joined[x, :, HS : HS + FFD] = (gate_in * sigma * up_in).astype(BF16)
    hid_ring = MpRing(net, joined, slice(HS, WOUTP))

    query = proj[:, :, 0:HS].reshape(BLK, HS) * in_scale
    query_scale = lax.rsqrt(jnp.mean(query * query, axis=-1, keepdims=True) + 1e-06)
    query_b = (query * query_scale).astype(BF16)
    dattended = (proj[:, :, WINP : WINP + HS].reshape(BLK, HS) * gate).astype(BF16)
    dhidden = proj[:, :, WINP + HS : PRW].reshape(BLK, 256)[:, 0:FFD] * gate
    dup = (dhidden * gate_in * sigma).astype(BF16)
    dgate_in = (dhidden * up_in * sigma * (1.0 + gate_in * (1.0 - sigma))).astype(BF16)
    dproj[x, :, 384:896] = jnp.concatenate([dgate_in, dup, jnp.zeros((BLK, 64), BF16)], axis=-1)

    row = lax.broadcasted_iota(jnp.int32, (BLK, 1), 0)
    row_z = row >> 5
    query_order = row_z * 128 + ((x + 8 - row_z) & 3) * 32 + (row & 31)
    col = lax.broadcasted_iota(jnp.int32, (1, ROWS), 1)
    col_z = (col >> 5) & 7
    key_order = col_z * 128 + (((col >> 8) + 8 - col_z) & 3) * 32 + (col & 31)
    visible = key_order <= query_order
    kv_gather.done()

    keys = kv[:, :, 0:HS].reshape(ROWS, HS)
    vals = kv[:, :, HS : 2 * HS].reshape(ROWS, HS)
    expo = jnp.where(visible, jnp.exp(dot_nt(query_b, keys) * FACTOR), 0.0)
    inverse = 1.0 / jnp.sum(expo, axis=-1, keepdims=True)
    joined[x, :, 0:HS] = (dot_nn(expo.astype(BF16), vals) * inverse).astype(BF16)
    att_gather = MpGather(net, joined, slice(0, HS))

    prob = expo * inverse
    dprob = dot_nt(dattended, vals)
    inner = jnp.sum(prob * dprob, axis=-1, keepdims=True)
    dscore = (prob * (dprob - inner)).astype(BF16)
    prob_b = prob.astype(BF16)
    dkey_part = (dot_tn(dscore, query_b) * FACTOR).astype(BF16)
    dvalue_part = dot_tn(prob_b, dattended).astype(BF16)
    for owner in range(NX):
        kg[owner, :, 0:HS] = dkey_part[owner * BLK : owner * BLK + BLK]
        kg[owner, :, HS : 2 * HS] = dvalue_part[owner * BLK : owner * BLK + BLK]
    kg_sum = MpSum(net, kg, kgl)
    hid_ring.pass_on()
    ff_ring = MpRing(net, dproj, slice(384, WINP))
    dquery_n = dot_nn(dscore, keys) * FACTOR

    def norm_back(values, scale, grads):
        return scale * grads - values * scale**3 * jnp.mean(grads * values, axis=-1, keepdims=True)

    dproj[x, :, 0:HS] = norm_back(query, query_scale, dquery_n).astype(BF16)
    att_gather.done()
    hid_ring.done()

    def rows_of(full, pair, columns):
        return full[:, pl.ds(pl.multiple_of(pair * 64, 64), 64)].reshape(BLK, columns)

    far_first = order[::-1]
    n_bufs = len(bufs) // 2
    delta_sum = SeqSum(
        net, bufs[:n_bufs], delta, lambda pair: dot_nn(rows_of(joined, pair, WOUTP), woutp[...]), far_first
    )
    dnormed_sum = SeqSum(
        net, bufs[n_bufs:], dnormed, lambda pair: dot_nn(rows_of(dproj, pair, WINP), winp[...]), far_first
    )
    delta_sum.multiply()
    key_grad = kg_sum.total()
    dproj[x, :, HS : 2 * HS] = norm_back(keyraw, key_scale, key_grad[:, 0:HS]).astype(BF16)
    dproj[x, :, 2 * HS : 3 * HS] = key_grad[:, HS : 2 * HS].astype(BF16)
    qkv_gather = MpGather(net, dproj, slice(0, 3 * HS))
    ff_ring.pass_on()
    delta_sum.turn()
    delta_sum.turn()
    ff_ring.done()
    qkv_gather.done()
    dnormed_sum.multiply()
    while delta_sum.turn():
        pass

    rows = g0[z, y, c].astype(F32)
    grads = g1[z, y, c].astype(F32)
    delta_b = delta[...].astype(BF16).astype(F32)
    small = lax.broadcasted_iota(jnp.int32, (CAP, 128), 1)

    def summed(which):
        return stats[which, 0] + stats[which, 1] + stats[which, 2] + stats[which, 3]

    def pick(tile, at):
        return jnp.sum(jnp.where(small == at, tile, 0.0), axis=-1, keepdims=True)

    def spread(which):
        own = fin.at[which, net.w]
        return [net.same(own, device) for device in (net.mate, net.cross, net.twin)]

    stats[1, 3] = row_sums((CAP, 128), (grads * delta_b,))
    arrive(*first_stats)
    tile = summed(0)
    in_scale = lax.rsqrt(pick(tile, 0) / D + 1e-05)
    gate = jax.nn.sigmoid(pick(tile, 1))
    fin[0, net.w] = (rows + gate * delta_b).astype(BF16)
    gate_stats = [net.send(stats.at[1, 3], stats.at[1, d], net.along_x[d]) for d in range(3)]
    copies = spread(0)
    while dnormed_sum.turn():
        pass
    dn = dnormed[...]
    stats[2, 3] = row_sums((CAP, 128), (dn * rows,))
    last_stats = [net.send(stats.at[2, 3], stats.at[2, d], net.along_x[d]) for d in range(3)]
    arrive(*gate_stats)
    dlogit = pick(summed(1), 0) * gate * (1.0 - gate)
    base = grads + dlogit * rw_ref[...]
    dn = in_scale * dn
    arrive(*copies)
    arrive(*last_stats)
    dinput = (dn - rows * in_scale**3 * (pick(summed(2), 0) / D)).astype(BF16).astype(F32)
    fin[1, net.w] = (base + dinput).astype(BF16)
    copies = spread(1)
    fin_out[0] = fin[0]
    arrive(*copies)
    fin_out[1] = fin[1]
    net.finish()


def place_kernel(sel_ref, fin_ref, res_ref, cot_ref, output_ref, grad_ref):
    sel = sel_ref[...]
    chosen = dot_tn(sel, jnp.ones((4 * CAP, 128), BF16))[:, 0:1] > 0.5
    for which, (source, target) in enumerate(((res_ref, output_ref), (cot_ref, grad_ref))):
        back = dot_tn(sel, fin_ref[which]).astype(BF16)
        target[...] = jnp.where(chosen, back, source[...])


def sum_scratch():
    return [
        pltpu.VMEM((2, NZ, NY, CAP, QD), BF16),
        pltpu.VMEM((NZ, NY, CAP, QD), BF16),
        pltpu.VMEM((NY, CAP, HALF), BF16),
        pltpu.VMEM((NZ, CAP, HALF), BF16),
        pltpu.VMEM((2, NZ // 2, NY, CAP, HALF // 2), BF16),
        pltpu.VMEM((2, NZ // 2, NY, CAP, HALF // 2), BF16),
        pltpu.VMEM((NY - 1, CAP, HALF), BF16),
        pltpu.VMEM((NY - 1, NZ, CAP, HALF), BF16),
        pltpu.VMEM((NZ - 1, CAP, HALF), BF16),
    ]


def local(residual, chosen_pos, chosen_count, router_weight, weight_in, weight_out, cotangent):
    n_sem = 320
    scratch = [
        pltpu.SemaphoreType.DMA((n_sem,)),
        pltpu.SemaphoreType.DMA((n_sem,)),
        pltpu.SemaphoreType.DMA((2,)),
        pltpu.VMEM((WINP, QD), BF16),
        pltpu.VMEM((WOUTP, QD), BF16),
        pltpu.VMEM((2, 8, 128), jnp.int32),
        pltpu.VMEM((2, 2, 2, CAP, QD), BF16),
        pltpu.VMEM((2, 2, CAP, QD), BF16),
        pltpu.VMEM((3, CAP, QD), BF16),
        pltpu.VMEM((NZ, NY, 2, CAP, QD), BF16),
        pltpu.VMEM((NZ, NY, 2, CAP, QD), BF16),
        pltpu.VMEM((4, NX, 2, 32, PRW), BF16),
        pltpu.VMEM((4, NX - 1, 2, 32, PRW), BF16),
        pltpu.VMEM((NZ, 32, PRW), F32),
        pltpu.VMEM((NX, BLK, 2 * HS), BF16),
        pltpu.VMEM((NX, BLK, WOUTP), BF16),
        pltpu.VMEM((NX, BLK, WINP), BF16),
        pltpu.VMEM((NX, BLK, 2 * HS), BF16),
        pltpu.VMEM((NX - 1, BLK, 2 * HS), BF16),
        pltpu.VMEM((CAP, QD), F32),
        pltpu.VMEM((CAP, QD), F32),
        pltpu.VMEM((3, 4, CAP, 128), F32),
        pltpu.VMEM((2, 4, CAP, QD), BF16),
    ] + sum_scratch() + sum_scratch()
    vmem = pl.BlockSpec(memory_space=pltpu.VMEM)
    anywhere = pl.BlockSpec(memory_space=pl.ANY)
    fin, sel = pl.pallas_call(
        kernel,
        out_shape=[
            jax.ShapeDtypeStruct((2, 4, CAP, QD), BF16),
            jax.ShapeDtypeStruct((4 * CAP, residual.shape[0]), BF16),
        ],
        in_specs=[vmem] * 5 + [anywhere] * 2,
        out_specs=[vmem] * 2,
        scratch_shapes=scratch,
        compiler_params=pltpu.CompilerParams(
            collective_id=0, has_side_effects=True, vmem_limit_bytes=62 * 1024 * 1024
        ),
        cost_estimate=pl.CostEstimate(flops=10**10, bytes_accessed=10**7, transcendentals=10**6),
    )(
        chosen_count[None, :], chosen_pos[None, :], residual, cotangent, router_weight[None, :],
        weight_in.T, weight_out,
    )
    fin = fin.reshape(2, 4 * CAP, QD)
    n_steps = 4
    tokens = residual.shape[0]
    columns = QD // n_steps
    block = pl.BlockSpec((tokens, columns), lambda i: (0, i))
    return pl.pallas_call(
        place_kernel,
        grid=(n_steps,),
        out_shape=[jax.ShapeDtypeStruct(residual.shape, BF16)] * 2,
        in_specs=[
            pl.BlockSpec((4 * CAP, tokens), lambda i: (0, 0)),
            pl.BlockSpec((2, 4 * CAP, columns), lambda i: (0, 0, i)),
            block,
            block,
        ],
        out_specs=[block, block],
    )(sel, fin, residual, cotangent)


def solution(mesh):
    spec = P("seq", "mp")
    return jax.shard_map(
        local,
        mesh=mesh,
        in_specs=(spec, P("seq"), P("seq"), P("mp"), P("mp", "seq"), spec, spec),
        out_specs=(spec, spec),
        check_vma=False,
    )
```

time: 177 us -> 178 us (level)
  Pallas kernels: 163 us -> 177 us
  local copies, waits for them, and re-layouts: 11.1 us -> 0 us
    pallas_call x1 -> x2, Pallas kernels: 163 us -> 177 us  [the longest x1 173 us: local(): pl.pallas_call(kernel, out_shape=[jax.ShapeDtypeStruct((2, 4, CAP, QD), B...]
    unnamed x3 -> x0, local copies, waits for them, and re-layouts: 9.8 us -> none
where the time goes in v2:
time: 178 us
  Pallas kernels  177 us (99%)
    pallas_call x1, Pallas kernels, local(): pl.pallas_call(kernel, out_shape=[jax.ShapeDtypeStruct((2, 4, CAP, QD), B...  173 us
    pallas_call x1, Pallas kernels, local(): pl.pallas_call(place_kernel, grid=(n_steps,), out_shape=[jax.ShapeDtypeSt...  4.1 us

profile of v2, /device:TPU:1, one launch (start us, length us, event | category | flops | bytes accessed | tf_op | source)
XLA Modules:
  0.0 178.2 jit_solution(3237819604398748087)
XLA Ops:
  1.3 172.8 %shard_map.86 = (bf16[2,4,16,2048]{3,2,1,0:T(8,128)(2,1)}, bf16[64,128]{1,0:T(8,128)(2,1)}) custom-call(s32[1,1]{1,0:T(1,128)} %bitcast.5.count_ref, s32[1,48]{1,0:T(1,128)} %bitcast.9, bf16[128,2048]{1,0:T(8,128)(2,1)} %res_ref.3, bf16[128,2048]{1,0:T(8,128)(2,1)} %cot_ref.3, f32[1,2048]{1,0:T(1,128)} %bitcast.8, bf16[832,2048]{1,0:T(8,128)(2,1)} %bitcast.7, ...), custom_call_target="tpu_custom_call" | custom-call | flops 10000000000 | bytes 10000000 | tf_op jit(solution)/shard_map/pallas_call | solution.py:655
  174.1 4.1 %shard_map.87 = (bf16[128,2048]{1,0:T(8,128)(2,1)}, bf16[128,2048]{1,0:T(8,128)(2,1)}) custom-call(bf16[64,128]{1,0:T(8,128)(2,1)} %get-tuple-element.4.sel_ref, bf16[2,64,2048]{2,1,0:T(8,128)(2,1)} %bitcast.6, bf16[128,2048]{1,0:T(8,128)(2,1)} %res_ref.3, bf16[128,2048]{1,0:T(8,128)(2,1)} %cot_ref.3), custom_call_target="tpu_custom_call" | custom-call | tf_op jit(solution)/shard_map/pallas_call | solution.py:677

commit v3 on v2

v3 whole, which is shorter than its diff:
```python
import jax
import jax.numpy as jnp
from jax import lax
from jax.experimental import pallas as pl
from jax.experimental.pallas import tpu as pltpu
from jax.sharding import PartitionSpec as P

MESH = pl.DeviceIdType.MESH
D = 8192
HS = 128
NZ, NY, NX = 8, 4, 4
CAP = 16
QD = D // NX
FFD = 224
WIN = 3 * HS + 2 * FFD
WINP = 896
WOUT = HS + FFD
WOUTP = 384
ROWS = 1024
BLK = 256
HALF = QD // 2
Z_FIRST = ((0, 512), (512, 256))
AW = 768
F32 = jnp.float32
BF16 = jnp.bfloat16
FACTOR = HS ** (-0.5)


def mod(value, n):
    return lax.rem(value + n, n)


def dot_nn(a, b):
    return jnp.dot(a, b, preferred_element_type=F32)


def dot_nt(a, b):
    return lax.dot_general(a, b, (((1,), (1,)), ((), ())), preferred_element_type=F32)


def dot_tn(a, b):
    return lax.dot_general(a, b, (((0,), (0,)), ((), ())), preferred_element_type=F32)


class Net:
    def __init__(self, send_sem, recv_sem):
        self.send_sem, self.recv_sem = send_sem, recv_sem
        self.used = 0
        self.sent = []
        seq = lax.axis_index("seq")
        x = self.x = lax.axis_index("mp")
        z = self.z = lax.div(seq, NY * 2)
        y = self.y = lax.rem(lax.div(seq, 2), NY)
        c = self.c = lax.rem(seq, 2)
        self.o = 1 - c
        self.upper = lax.rem(y, 2)
        self.w = self.upper * 2 + c
        yw = y + 1 - 2 * self.upper
        yo = mod(y - 1 + 2 * self.upper, NY)
        self.twin = self.at(z, y, self.o, x)
        self.mate = self.at(z, yw, c, x)
        self.cross = self.at(z, yw, self.o, x)
        self.beyond = self.at(z, yo, c, x)
        self.along_x = [self.at(z, y, c, mod(x + d, NX)) for d in range(1, NX)]
        self.along_y = [self.at(z, mod(y + d, NY), c, x) for d in range(1, NY)]
        self.along_z = [self.at(mod(z + d, NZ), y, c, x) for d in range(1, NZ)]
        self.xp, self.xm = self.along_x[0], self.along_x[-1]
        self.yp, self.ym = self.along_y[0], self.along_y[-1]
        self.zp, self.zm = self.along_z[0], self.along_z[-1]

    def at(self, z, y, c, x):
        return ((z * NY + y) * 2 + c, x)

    def enter(self):
        barrier = pltpu.get_barrier_semaphore()
        partners = [self.twin, self.cross] + self.along_x + self.along_y + self.along_z
        for partner in partners:
            pl.semaphore_signal(barrier, inc=1, device_id=partner, device_id_type=MESH)
        pl.semaphore_wait(barrier, len(partners))

    def group(self, copies, whole):
        send_sem, recv_sem = self.send_sem.at[self.used], self.recv_sem.at[self.used]
        self.used += 1
        for src, dst, device in copies:
            pltpu.make_async_remote_copy(
                src_ref=src, dst_ref=dst, send_sem=send_sem, recv_sem=recv_sem, device_id=device, device_id_type=MESH
            ).start()
        self.sent.append(pltpu.make_async_copy(whole, whole, send_sem))
        return pltpu.make_async_copy(whole, whole, recv_sem)

    def send(self, src, dst, device):
        return self.group([(src, dst, device)], dst)

    def same(self, ref, device):
        return self.send(ref, ref, device)

    def finish(self):
        assert self.used == self.send_sem.shape[0], self.used
        for copy in self.sent:
            copy.wait()


def arrive(*copies):
    for copy in copies:
        copy.wait()


class MpSum:
    def __init__(self, net, part, landed):
        self.net, self.part, self.landed = net, part, landed
        self.copy = net.group(
            [(part.at[mod(net.x + d, NX)], landed.at[d - 1], net.along_x[d - 1]) for d in range(1, NX)], landed
        )

    def total(self):
        arrive(self.copy)
        total = self.part[self.net.x].astype(F32)
        for d in range(NX - 1):
            total = total + self.landed[d].astype(F32)
        return total


class MpGather:
    def __init__(self, net, full, lanes):
        block = full.at[net.x, :, lanes]
        self.copy = net.group([(block, block, device) for device in net.along_x], full.at[0 : NX - 1, :, lanes])

    def done(self):
        arrive(self.copy)


class MpRing:
    def __init__(self, net, full, lanes):
        self.net, self.full, self.lanes = net, full, lanes
        block = full.at[net.x, :, lanes]
        self.copy = net.group([(block, block, net.xp), (block, block, net.xm)], full.at[0:2, :, lanes])

    def pass_on(self):
        net = self.net
        arrive(self.copy)
        left = self.full.at[mod(net.x - 1, NX), 0 : BLK // 2, self.lanes]
        right = self.full.at[mod(net.x + 1, NX), BLK // 2 : BLK, self.lanes]
        self.copy = net.group([(left, left, net.xp), (right, right, net.xm)], self.full.at[0, :, self.lanes])

    def done(self):
        arrive(self.copy)


def chain(net, pos, block, from_left, from_right, width):
    hops = NZ // 2
    half = width // 2
    far = mod(pos + hops, NZ)
    copy = net.group(
        [
            (block(far, 0, half), from_left.at[0, ..., 0:half], net.zp),
            (block(far, half, width), from_right.at[0, ..., half:width], net.zm),
        ],
        from_left.at[0],
    )
    yield
    for step in range(1, hops):
        right, left = mod(pos + hops - step, NZ), mod(pos - hops + step, NZ)
        arrive(copy)
        for at, landed, (lo, hi) in ((right, from_left, (0, half)), (left, from_right, (half, width))):
            if step > 1:
                lo, hi = 0, width
            target = block(at, lo, hi)
            target[...] = (target[...].astype(F32) + landed[step - 1, ..., lo:hi].astype(F32)).astype(BF16)
        copy = net.group(
            [
                (block(right, 0, width), from_left.at[step], net.zp),
                (block(left, 0, width), from_right.at[step], net.zm),
            ],
            from_left.at[0:2],
        )
        yield
    arrive(copy)


class SeqSum:
    def __init__(self, net, bufs, out, product, order):
        self.net, self.bufs, self.out, self.product, self.order = net, bufs, out, product, order
        self.by_copies, self.by_all = [], []
        self.steps = [self.along_z_first(0), self.along_z_first(1)]

    def multiply(self, eager):
        net, part, other = self.net, self.bufs[0], self.bufs[1]
        self.copies = []
        for k, pair in enumerate(self.order):
            rows = self.product(pair)
            for owner in range(NX):
                for place in range(2):
                    z = 2 * pair + place
                    y = lax.rem(owner - z + 2 * NZ, NY)
                    for core in range(2):
                        at = ((owner * 2 + place) * 2 + core) * CAP
                        part[core, z, y] = rows[at : at + CAP].astype(BF16)
            both = pl.ds(2 * pair, 2)
            self.copies.append(net.send(part.at[net.o, both], other.at[both], net.twin))
            if k:
                self.merge(k - 1)
            if k == 3 and eager:
                self.turn()
        self.merge(len(self.order) - 1)
        self.steps.append(self.along_y_first())

    def merge(self, k):
        net, part, other, byl = self.net, self.bufs[0], self.bufs[1], self.bufs[9]
        arrive(self.copies[k])
        pair = self.order[k]
        for place in range(2):
            z = 2 * pair + place
            part[net.c, z] = (part[net.c, z].astype(F32) + other[z].astype(F32)).astype(BF16)
        if k == 0:
            for step in self.steps:
                next(step)
        both = pl.ds(2 * pair, 2)
        for d in range(1, NY):
            source = part.at[net.c, both, mod(net.y + d, NY), :, AW:QD]
            self.by_copies.append((source, byl.at[d - 1, both], net.along_y[d - 1]))
        self.by = net.group(self.by_copies, byl.at[:, 0:2])
        self.by_copies = []
        self.by_all.append(self.by)

    def turn(self):
        left = []
        for step in self.steps:
            try:
                next(step)
                left.append(step)
            except StopIteration:
                pass
        self.steps = left
        return bool(left)

    def along_z_first(self, which):
        net, part, qa, ayl = self.net, self.bufs[0], self.bufs[2], self.bufs[8]
        first, width = Z_FIRST[which]
        left, right = self.bufs[4 + 2 * which], self.bufs[5 + 2 * which]
        block = lambda t, lo, hi: part.at[net.c, t, :, :, first + lo : first + hi]
        yield from chain(net, net.z, block, left, right, width)
        last = NZ // 2 - 1
        lanes = slice(first, first + width)
        qa[:, :, lanes] = (
            part[net.c, net.z, :, :, lanes].astype(F32) + left[last].astype(F32) + right[last].astype(F32)
        ).astype(BF16)
        copy = net.group(
            [
                (qa.at[mod(net.y + d, NY), :, lanes], ayl.at[d - 1, :, lanes], net.along_y[d - 1])
                for d in range(1, NY)
            ],
            ayl.at[:, :, lanes],
        )
        yield
        arrive(copy)
        total = qa[net.y, :, lanes].astype(F32)
        for d in range(NY - 1):
            total = total + ayl[d, :, lanes].astype(F32)
        self.out[:, lanes] = total

    def along_y_first(self):
        net, part, qb, byl, bzl = self.net, self.bufs[0], self.bufs[3], self.bufs[9], self.bufs[10]
        arrive(*self.by_all)
        total = part[net.c, :, net.y, :, AW:QD].astype(F32)
        for d in range(NY - 1):
            total = total + byl[d].astype(F32)
        qb[...] = total.astype(BF16)
        copy = net.group(
            [(qb.at[mod(net.z + d, NZ)], bzl.at[d - 1], net.along_z[d - 1]) for d in range(1, NZ)], bzl
        )
        yield
        arrive(copy)
        total = qb[net.z].astype(F32)
        for d in range(NZ - 1):
            total = total + bzl[d].astype(F32)
        self.out[:, AW:QD] = total


def row_sums(tile, columns):
    small = lax.broadcasted_iota(jnp.int32, tile, 1)
    result = jnp.zeros(tile, F32)
    for at, product in enumerate(columns):
        result = jnp.where(small == at, jnp.sum(product, axis=-1, keepdims=True), result)
    return result


def kernel(
    count_ref, pos_ref, res_ref, cot_ref, rw_ref, win_ref, wout_ref,
    fin_out, sel_out,
    send_sem, recv_sem, load_sem, winp, woutp, counts, contrib, from_twin, from_mate, g0, g1,
    pr, prl, pd, pdl, proj, dj, kv, joined, dproj, kg, kgl,
    delta, dnormed, stats, fin, *bufs,
):
    net = Net(send_sem, recv_sem)
    x, y, z, c = net.x, net.y, net.z, net.c
    loads = (
        pltpu.make_async_copy(win_ref, winp.at[0:WIN], load_sem.at[0]),
        pltpu.make_async_copy(wout_ref, woutp.at[0:WOUT], load_sem.at[1]),
    )
    for load in loads:
        load.start()
    net.enter()

    counts[0] = jnp.zeros((8, 128), jnp.int32) + count_ref[...]
    arrive(net.send(counts.at[0], counts.at[1], net.twin))
    n_slots = pos_ref.shape[1]
    mine, twins = counts[0, 0:1, 0:n_slots], counts[1, 0:1, 0:n_slots]
    before = twins * c + (4 * CAP - mine - twins) * net.upper
    row = lax.broadcasted_iota(jnp.int32, (4 * CAP, n_slots), 0)
    slot = lax.broadcasted_iota(jnp.int32, (4 * CAP, n_slots), 1)
    place_of = jnp.where(row - slot == before, F32(1.0), F32(0.0)).astype(BF16)
    token = lax.broadcasted_iota(jnp.int32, (128, n_slots), 0)
    slot = lax.broadcasted_iota(jnp.int32, (128, n_slots), 1)
    token_of = jnp.where((token == pos_ref[...]) & (slot < mine), F32(1.0), F32(0.0)).astype(BF16)
    sel = dot_nt(place_of, token_of).astype(BF16)
    sel_out[...] = sel

    copies = []
    for which, source in enumerate((res_ref, cot_ref)):
        rows = dot_nn(sel, source[...]).astype(BF16)
        for chip in range(2):
            for core in range(2):
                at = (chip * 2 + core) * CAP
                contrib[which, core, chip] = rows[at : at + CAP]
        copies.append(net.send(contrib.at[which, net.o], from_twin.at[which], net.twin))
    for which in range(2):
        arrive(copies[which])
        contrib[which, c] = (contrib[which, c].astype(F32) + from_twin[which].astype(F32)).astype(BF16)
        if which == 0:
            r_copy = net.send(contrib.at[0, c], from_mate.at[0:2], net.mate)
        else:
            d_copy = net.send(contrib.at[1, c, 1 - net.upper], from_mate.at[2], net.mate)
    mine_q = lax.div(y, 2)
    arrive(r_copy)
    for place in range(2):
        g0[z, 2 * mine_q + place, c] = (
            contrib[0, c, place].astype(F32) + from_mate[place].astype(F32)
        ).astype(BF16)

    def both_ways(step, g, ys, few):
        near, far = mod(z - step + 1, NZ), mod(z + step - 1, NZ)
        if step < 4:
            right, left = g.at[near, ys, c], g.at[far, ys, c]
            whole = g.at[0:2, few, 0]
        else:
            right, left = g.at[near, ys, c, :, 0:HALF], g.at[far, ys, c, :, HALF:QD]
            whole = g.at[0, few, 0]
        return net.group([(right, right, net.zp), (left, left, net.zm)], whole)

    def r_ring(step, q):
        return both_ways(step, g0, pl.ds(2 * q, 2), slice(0, 2))

    def d_ring(step):
        return both_ways(step, g1, y, 0)

    def d_out(*ds):
        result = []
        for d in ds:
            block = g1.at[mod(z + d, NZ), y, c]
            result.append((d, net.group([(block, block, device) for device in net.along_y], g1.at[0, 0:3, 0])))
        return result

    def d_twin(items):
        result = []
        for d, copy in items:
            arrive(copy)
            result.append(net.same(g1.at[mod(z + d, NZ), :, c], net.twin))
        return result

    def r_twin(*ds):
        return [net.same(g0.at[mod(z + d, NZ), :, c], net.twin) for d in ds]

    lane = lax.broadcasted_iota(jnp.int32, (BLK, 128), 1)

    def rows_at(g, ds):
        rows = [g[mod(z + d, NZ)].reshape(BLK // 2, QD) for d in ds]
        return rows[0] if len(ds) == 1 else jnp.concatenate(rows, axis=0)

    def hand_out(part, ds, result, columns):
        for i, d in enumerate(ds):
            at = mod(z + d, NZ)
            for row in range(NY):
                owner = lax.rem(at + row, NX)
                part[at, owner, :, columns] = result[(i * NY + row) * 32 : (i * NY + row) * 32 + 32]

    def in_stage(*ds):
        rows = rows_at(g0, ds)
        result = dot_nt(rows, winp[...])
        rows_f = rows.astype(F32)
        tail = result[:, 768:896]
        at = WIN - 768
        for value in (
            jnp.sum(rows_f * rows_f, axis=-1, keepdims=True),
            jnp.sum(rows_f * rw_ref[...], axis=-1, keepdims=True),
        ):
            for _ in range(3):
                rounded = value.astype(BF16).astype(F32)
                tail = jnp.where(lane[0 : rows.shape[0]] == at, rounded, tail)
                value = value - rounded
                at += 1
        hand_out(pr, ds, result[:, 0:768].astype(BF16), slice(0, 768))
        hand_out(pr, ds, tail.astype(BF16), slice(768, WINP))
        return [(mod(z + d, NZ), MpSum(net, pr.at[mod(z + d, NZ)], prl.at[mod(z + d, NZ)])) for d in ds]

    def back_stage(*ds):
        hand_out(pd, ds, dot_nt(rows_at(g1, ds), woutp[...]).astype(BF16), slice(0, WOUTP))
        return [(mod(z + d, NZ), MpSum(net, pd.at[mod(z + d, NZ)], pdl.at[mod(z + d, NZ)])) for d in ds]

    def collect(target, items):
        for at, part in items:
            target[at] = part.total()

    other_q = 1 - mine_q
    p_ring = r_ring(1, mine_q)
    r_copy = net.same(g0.at[z, pl.ds(2 * mine_q, 2), c], net.beyond)
    arrive(d_copy)
    g1[z, y, c] = (contrib[1, c, net.upper].astype(F32) + from_mate[2].astype(F32)).astype(BF16)
    g_ring = d_ring(1)
    d_0 = d_out(0)
    rows = g0[z, y, c].astype(F32)
    stats[0, 3] = row_sums((CAP, 128), (rows * rows, rows * rw_ref[...]))

    def stats_out(which):
        return net.group(
            [(stats.at[which, 3], stats.at[which, d], net.along_x[d]) for d in range(3)], stats.at[which, 0:3]
        )

    first_stats = stats_out(0)
    winp[WIN:WINP] = jnp.zeros((WINP - WIN, QD), BF16)
    woutp[WOUT:WOUTP] = jnp.zeros((WOUTP - WOUT, QD), BF16)
    for load in loads:
        load.wait()
    arrive(r_copy)
    q_ring = r_ring(1, other_q)
    r_0 = r_twin(0)
    arrive(g_ring)
    g_ring = d_ring(2)
    d_1 = d_out(1, -1)
    arrive(p_ring)
    p_ring = r_ring(2, mine_q)
    arrive(*r_0)
    in_0 = in_stage(0)
    arrive(q_ring)
    q_ring = r_ring(2, other_q)
    r_1 = r_twin(1, -1)
    arrive(g_ring)
    g_ring = d_ring(3)
    d_2 = d_out(2, -2)
    d_0 = d_twin(d_0)
    arrive(p_ring)
    p_ring = r_ring(3, mine_q)
    arrive(*r_1)
    in_1 = in_stage(1, -1)
    arrive(q_ring)
    q_ring = r_ring(3, other_q)
    r_2 = r_twin(2, -2)
    d_1 = d_twin(d_1)
    arrive(g_ring)
    g_ring = d_ring(4)
    d_3 = d_out(3, -3)
    arrive(p_ring)
    p_ring = r_ring(4, mine_q)
    arrive(*r_2)
    in_2 = in_stage(2, -2)
    arrive(q_ring)
    q_ring = r_ring(4, other_q)
    r_3 = r_twin(3, -3)
    d_2 = d_twin(d_2)
    arrive(*d_0)
    back_0 = back_stage(0)
    arrive(g_ring)
    d_4 = d_out(4)
    arrive(*r_3)
    in_3 = in_stage(3, -3)
    arrive(p_ring, q_ring)
    r_4 = r_twin(4)
    collect(proj, in_0)
    collect(proj, in_1)
    arrive(*r_4)
    in_4 = in_stage(4)
    arrive(*d_1)
    back_1 = back_stage(1, -1)
    d_3 = d_twin(d_3)
    collect(proj, in_2)
    collect(proj, in_3)
    d_4 = d_twin(d_4)
    collect(proj, in_4)

    tail = proj[:, :, 768:896].reshape(BLK, 128)
    at = WIN - 768
    square = jnp.sum(jnp.where((lane >= at) & (lane < at + 3), tail, 0.0), axis=-1, keepdims=True)
    logit = jnp.sum(jnp.where((lane >= at + 3) & (lane < at + 6), tail, 0.0), axis=-1, keepdims=True)
    in_scale = lax.rsqrt(square / D + 1e-05)
    gate = jax.nn.sigmoid(logit)
    keyraw = proj[:, :, HS : 2 * HS].reshape(BLK, HS) * in_scale
    key_scale = lax.rsqrt(jnp.mean(keyraw * keyraw, axis=-1, keepdims=True) + 1e-06)
    kv[x, :, 0:HS] = (keyraw * key_scale).astype(BF16)
    kv[x, :, HS : 2 * HS] = (proj[:, :, 2 * HS : 3 * HS].reshape(BLK, HS) * in_scale).astype(BF16)
    kv_gather = MpGather(net, kv, slice(0, 2 * HS))

    gate_up = proj[:, :, 384:896].reshape(BLK, 512) * in_scale
    gate_in = gate_up[:, 0:FFD]
    up_in = gate_up[:, FFD : 2 * FFD]
    sigma = jax.nn.sigmoid(gate_in)
    joined[x, :, 256:384] = jnp.zeros((BLK, 128), BF16)
    joined[x, :, HS : HS + FFD] = (gate_in * sigma * up_in).astype(BF16)
    hid_ring = MpRing(net, joined, slice(HS, WOUTP))

    arrive(*d_2)
    back_2 = back_stage(2, -2)
    arrive(*d_3)
    back_3 = back_stage(3, -3)
    arrive(*d_4)
    back_4 = back_stage(4)
    query = proj[:, :, 0:HS].reshape(BLK, HS) * in_scale
    query_scale = lax.rsqrt(jnp.mean(query * query, axis=-1, keepdims=True) + 1e-06)
    query_b = (query * query_scale).astype(BF16)
    row = lax.broadcasted_iota(jnp.int32, (BLK, 1), 0)
    row_z = row >> 5
    query_order = row_z * 128 + ((x + 8 - row_z) & 3) * 32 + (row & 31)
    col = lax.broadcasted_iota(jnp.int32, (1, ROWS), 1)
    col_z = (col >> 5) & 7
    key_order = col_z * 128 + (((col >> 8) + 8 - col_z) & 3) * 32 + (col & 31)
    visible = key_order <= query_order
    kv_gather.done()

    keys = kv[:, :, 0:HS].reshape(ROWS, HS)
    vals = kv[:, :, HS : 2 * HS].reshape(ROWS, HS)
    expo = jnp.where(visible, jnp.exp(dot_nt(query_b, keys) * FACTOR), 0.0)
    inverse = 1.0 / jnp.sum(expo, axis=-1, keepdims=True)
    joined[x, :, 0:HS] = (dot_nn(expo.astype(BF16), vals) * inverse).astype(BF16)
    att_gather = MpGather(net, joined, slice(0, HS))

    for items in (back_0, back_1, back_2, back_3, back_4):
        collect(dj, items)
    dattended = (dj[:, :, 0:HS].reshape(BLK, HS) * gate).astype(BF16)
    dhidden = dj[:, :, HS:WOUTP].reshape(BLK, 256)[:, 0:FFD] * gate
    dup = (dhidden * gate_in * sigma).astype(BF16)
    dgate_in = (dhidden * up_in * sigma * (1.0 + gate_in * (1.0 - sigma))).astype(BF16)
    dproj[x, :, 384:896] = jnp.concatenate([dgate_in, dup, jnp.zeros((BLK, 64), BF16)], axis=-1)

    prob = expo * inverse
    dprob = dot_nt(dattended, vals)
    inner = jnp.sum(prob * dprob, axis=-1, keepdims=True)
    dscore = (prob * (dprob - inner)).astype(BF16)
    prob_b = prob.astype(BF16)
    dkey_part = (dot_tn(dscore, query_b) * FACTOR).astype(BF16)
    dvalue_part = dot_tn(prob_b, dattended).astype(BF16)
    for owner in range(NX):
        kg[owner, :, 0:HS] = dkey_part[owner * BLK : owner * BLK + BLK]
        kg[owner, :, HS : 2 * HS] = dvalue_part[owner * BLK : owner * BLK + BLK]
    kg_sum = MpSum(net, kg, kgl)
    hid_ring.pass_on()
    ff_ring = MpRing(net, dproj, slice(384, WINP))
    dquery_n = dot_nn(dscore, keys) * FACTOR

    def norm_back(values, scale, grads):
        return scale * grads - values * scale**3 * jnp.mean(grads * values, axis=-1, keepdims=True)

    dproj[x, :, 0:HS] = norm_back(query, query_scale, dquery_n).astype(BF16)
    key_grad = kg_sum.total()
    dproj[x, :, HS : 2 * HS] = norm_back(keyraw, key_scale, key_grad[:, 0:HS]).astype(BF16)
    dproj[x, :, 2 * HS : 3 * HS] = key_grad[:, HS : 2 * HS].astype(BF16)
    qkv_gather = MpGather(net, dproj, slice(0, 3 * HS))
    att_gather.done()
    hid_ring.done()

    def rows_of(full, pair, columns):
        return full[:, pl.ds(pl.multiple_of(pair * 64, 64), 64)].reshape(BLK, columns)

    pair = lax.div(z, 2)
    turned = 1 - 2 * lax.rem(z, 2)
    far_first = (mod(pair + 2, 4), mod(pair + turned, 4), mod(pair - turned, 4), pair)
    n_bufs = len(bufs) // 2
    delta_sum = SeqSum(
        net, bufs[:n_bufs], delta, lambda pair: dot_nn(rows_of(joined, pair, WOUTP), woutp[...]), far_first
    )
    dnormed_sum = SeqSum(
        net, bufs[n_bufs:], dnormed, lambda pair: dot_nn(rows_of(dproj, pair, WINP), winp[...]), far_first
    )
    ff_ring.pass_on()
    delta_sum.multiply(False)
    delta_sum.turn()
    ff_ring.done()
    qkv_gather.done()
    delta_sum.turn()
    dnormed_sum.multiply(True)
    while delta_sum.turn():
        dnormed_sum.turn()

    rows = g0[z, y, c].astype(F32)
    grads = g1[z, y, c].astype(F32)
    delta_b = delta[...].astype(BF16).astype(F32)
    small = lax.broadcasted_iota(jnp.int32, (CAP, 128), 1)

    def summed(which):
        return stats[which, 0] + stats[which, 1] + stats[which, 2] + stats[which, 3]

    def pick(tile, at):
        return jnp.sum(jnp.where(small == at, tile, 0.0), axis=-1, keepdims=True)

    def spread(which):
        own = fin.at[which, net.w]
        return net.group([(own, own, device) for device in (net.mate, net.cross, net.twin)], fin.at[which, 0:3])

    stats[1, 3] = row_sums((CAP, 128), (grads * delta_b,))
    arrive(first_stats)
    tile = summed(0)
    in_scale = lax.rsqrt(pick(tile, 0) / D + 1e-05)
    gate = jax.nn.sigmoid(pick(tile, 1))
    fin[0, net.w] = (rows + gate * delta_b).astype(BF16)
    gate_stats = stats_out(1)
    first_rows = spread(0)
    while dnormed_sum.turn():
        pass
    dn = dnormed[...]
    stats[2, 3] = row_sums((CAP, 128), (dn * rows,))
    last_stats = stats_out(2)
    arrive(gate_stats)
    dlogit = pick(summed(1), 0) * gate * (1.0 - gate)
    base = grads + dlogit * rw_ref[...]
    dn = in_scale * dn
    arrive(first_rows, last_stats)
    dinput = (dn - rows * in_scale**3 * (pick(summed(2), 0) / D)).astype(BF16).astype(F32)
    fin[1, net.w] = (base + dinput).astype(BF16)
    last_rows = spread(1)
    fin_out[0] = fin[0]
    arrive(last_rows)
    fin_out[1] = fin[1]
    net.finish()


def place_kernel(sel_ref, fin_ref, res_ref, cot_ref, output_ref, grad_ref):
    sel = sel_ref[...]
    chosen = dot_tn(sel, jnp.ones((4 * CAP, 128), BF16))[:, 0:1] > 0.5
    for which, (source, target) in enumerate(((res_ref, output_ref), (cot_ref, grad_ref))):
        back = dot_tn(sel, fin_ref[which]).astype(BF16)
        target[...] = jnp.where(chosen, back, source[...])


def sum_scratch():
    return [
        pltpu.VMEM((2, NZ, NY, CAP, QD), BF16),
        pltpu.VMEM((NZ, NY, CAP, QD), BF16),
        pltpu.VMEM((NY, CAP, AW), BF16),
        pltpu.VMEM((NZ, CAP, QD - AW), BF16),
        pltpu.VMEM((NZ // 2, NY, CAP, Z_FIRST[0][1]), BF16),
        pltpu.VMEM((NZ // 2, NY, CAP, Z_FIRST[0][1]), BF16),
        pltpu.VMEM((NZ // 2, NY, CAP, Z_FIRST[1][1]), BF16),
        pltpu.VMEM((NZ // 2, NY, CAP, Z_FIRST[1][1]), BF16),
        pltpu.VMEM((NY - 1, CAP, AW), BF16),
        pltpu.VMEM((NY - 1, NZ, CAP, QD - AW), BF16),
        pltpu.VMEM((NZ - 1, CAP, QD - AW), BF16),
    ]


def local(residual, chosen_pos, chosen_count, router_weight, weight_in, weight_out, cotangent):
    n_sem = 109
    scratch = [
        pltpu.SemaphoreType.DMA((n_sem,)),
        pltpu.SemaphoreType.DMA((n_sem,)),
        pltpu.SemaphoreType.DMA((2,)),
        pltpu.VMEM((WINP, QD), BF16),
        pltpu.VMEM((WOUTP, QD), BF16),
        pltpu.VMEM((2, 8, 128), jnp.int32),
        pltpu.VMEM((2, 2, 2, CAP, QD), BF16),
        pltpu.VMEM((2, 2, CAP, QD), BF16),
        pltpu.VMEM((3, CAP, QD), BF16),
        pltpu.VMEM((NZ, NY, 2, CAP, QD), BF16),
        pltpu.VMEM((NZ, NY, 2, CAP, QD), BF16),
        pltpu.VMEM((NZ, NX, 32, WINP), BF16),
        pltpu.VMEM((NZ, NX - 1, 32, WINP), BF16),
        pltpu.VMEM((NZ, NX, 32, WOUTP), BF16),
        pltpu.VMEM((NZ, NX - 1, 32, WOUTP), BF16),
        pltpu.VMEM((NZ, 32, WINP), F32),
        pltpu.VMEM((NZ, 32, WOUTP), F32),
        pltpu.VMEM((NX, BLK, 2 * HS), BF16),
        pltpu.VMEM((NX, BLK, WOUTP), BF16),
        pltpu.VMEM((NX, BLK, WINP), BF16),
        pltpu.VMEM((NX, BLK, 2 * HS), BF16),
        pltpu.VMEM((NX - 1, BLK, 2 * HS), BF16),
        pltpu.VMEM((CAP, QD), F32),
        pltpu.VMEM((CAP, QD), F32),
        pltpu.VMEM((3, 4, CAP, 128), F32),
        pltpu.VMEM((2, 4, CAP, QD), BF16),
    ] + sum_scratch() + sum_scratch()
    vmem = pl.BlockSpec(memory_space=pltpu.VMEM)
    anywhere = pl.BlockSpec(memory_space=pl.ANY)
    fin, sel = pl.pallas_call(
        kernel,
        out_shape=[
            jax.ShapeDtypeStruct((2, 4, CAP, QD), BF16),
            jax.ShapeDtypeStruct((4 * CAP, residual.shape[0]), BF16),
        ],
        in_specs=[vmem] * 5 + [anywhere] * 2,
        out_specs=[vmem] * 2,
        scratch_shapes=scratch,
        compiler_params=pltpu.CompilerParams(
            collective_id=0, has_side_effects=True, vmem_limit_bytes=62 * 1024 * 1024
        ),
        cost_estimate=pl.CostEstimate(flops=10**10, bytes_accessed=10**7, transcendentals=10**6),
    )(
        chosen_count[None, :], chosen_pos[None, :], residual, cotangent, router_weight[None, :],
        weight_in.T, weight_out,
    )
    fin = fin.reshape(2, 4 * CAP, QD)
    n_steps = 1
    tokens = residual.shape[0]
    columns = QD // n_steps
    block = pl.BlockSpec((tokens, columns), lambda i: (0, i))
    return pl.pallas_call(
        place_kernel,
        grid=(n_steps,),
        out_shape=[jax.ShapeDtypeStruct(residual.shape, BF16)] * 2,
        in_specs=[
            pl.BlockSpec((4 * CAP, tokens), lambda i: (0, 0)),
            pl.BlockSpec((2, 4 * CAP, columns), lambda i: (0, 0, i)),
            block,
            block,
        ],
        out_specs=[block, block],
    )(sel, fin, residual, cotangent)


def solution(mesh):
    spec = P("seq", "mp")
    return jax.shard_map(
        local,
        mesh=mesh,
        in_specs=(spec, P("seq"), P("seq"), P("mp"), P("mp", "seq"), spec, spec),
        out_specs=(spec, spec),
        check_vma=False,
    )
```

time: 178 us -> 171 us (0.961)
  Pallas kernels: 177 us -> 170 us
    pallas_call x1, Pallas kernels: 173 us -> 167 us  [local(): pl.pallas_call(kernel, out_shape=[jax.ShapeDtypeStruct((2, 4, CAP, QD), B...]
where the time goes in v3:
time: 171 us
  Pallas kernels  170 us (99%)
    pallas_call x1, Pallas kernels, local(): pl.pallas_call(kernel, out_shape=[jax.ShapeDtypeStruct((2, 4, CAP, QD), B...  167 us

profile of v3, /device:TPU:1, one launch (start us, length us, event | category | flops | bytes accessed | tf_op | source)
XLA Modules:
  0.0 171.1 jit_solution(12739778169192171415)
XLA Ops:
  1.3 167.1 %shard_map.86 = (bf16[2,4,16,2048]{3,2,1,0:T(8,128)(2,1)}, bf16[64,128]{1,0:T(8,128)(2,1)}) custom-call(s32[1,1]{1,0:T(1,128)} %bitcast.5.count_ref, s32[1,48]{1,0:T(1,128)} %bitcast.9, bf16[128,2048]{1,0:T(8,128)(2,1)} %res_ref.3, bf16[128,2048]{1,0:T(8,128)(2,1)} %cot_ref.3, f32[1,2048]{1,0:T(1,128)} %bitcast.8, bf16[832,2048]{1,0:T(8,128)(2,1)} %bitcast.7, ...), custom_call_target="tpu_custom_call" | custom-call | flops 10000000000 | bytes 10000000 | tf_op jit(solution)/shard_map/pallas_call | solution.py:689
  168.4 2.7 %shard_map.87 = (bf16[128,2048]{1,0:T(8,128)(2,1)}, bf16[128,2048]{1,0:T(8,128)(2,1)}) custom-call(bf16[64,128]{1,0:T(8,128)(2,1)} %get-tuple-element.4.sel_ref, bf16[2,64,2048]{2,1,0:T(8,128)(2,1)} %bitcast.6, bf16[128,2048]{1,0:T(8,128)(2,1)} %res_ref.3, bf16[128,2048]{1,0:T(8,128)(2,1)} %cot_ref.3), custom_call_target="tpu_custom_call" | custom-call | tf_op jit(solution)/shard_map/pallas_call | solution.py:711

commit v4 on v3

--- a/solution.py
+++ b/solution.py
@@ -120,10 +120,22 @@
         return total
 
 
+def rows_of_owner(full, owner, lanes, first=0, last=NZ):
+    return [full.at[at, lax.rem(owner - at + NZ, NX), :, lanes] for at in range(first, last)]
+
+
+def give(net, full, lanes, rows):
+    for at in range(NZ):
+        full[at, lax.rem(net.x - at + NZ, NX), :, lanes] = rows[at * 32 : at * 32 + 32]
+
+
 class MpGather:
     def __init__(self, net, full, lanes):
-        block = full.at[net.x, :, lanes]
-        self.copy = net.group([(block, block, device) for device in net.along_x], full.at[0 : NX - 1, :, lanes])
+        blocks = rows_of_owner(full, net.x, lanes)
+        self.copy = net.group(
+            [(block, block, device) for device in net.along_x for block in blocks],
+            full.at[0 : NZ // NX * (NX - 1), :, :, lanes],
+        )
 
     def done(self):
         arrive(self.copy)
@@ -132,15 +144,21 @@
 class MpRing:
     def __init__(self, net, full, lanes):
         self.net, self.full, self.lanes = net, full, lanes
-        block = full.at[net.x, :, lanes]
-        self.copy = net.group([(block, block, net.xp), (block, block, net.xm)], full.at[0:2, :, lanes])
+        blocks = rows_of_owner(full, net.x, lanes)
+        self.copy = net.group(
+            [(block, block, device) for device in (net.xp, net.xm) for block in blocks],
+            full.at[0 : NZ // 2, :, :, lanes],
+        )
 
     def pass_on(self):
         net = self.net
         arrive(self.copy)
-        left = self.full.at[mod(net.x - 1, NX), 0 : BLK // 2, self.lanes]
-        right = self.full.at[mod(net.x + 1, NX), BLK // 2 : BLK, self.lanes]
-        self.copy = net.group([(left, left, net.xp), (right, right, net.xm)], self.full.at[0, :, self.lanes])
+        left = rows_of_owner(self.full, mod(net.x - 1, NX), self.lanes, 0, NZ // 2)
+        right = rows_of_owner(self.full, mod(net.x + 1, NX), self.lanes, NZ // 2, NZ)
+        self.copy = net.group(
+            [(block, block, net.xp) for block in left] + [(block, block, net.xm) for block in right],
+            self.full.at[0 : NZ // NX, :, :, self.lanes],
+        )
 
     def done(self):
         arrive(self.copy)
@@ -188,13 +206,11 @@
         self.copies = []
         for k, pair in enumerate(self.order):
             rows = self.product(pair)
-            for owner in range(NX):
-                for place in range(2):
-                    z = 2 * pair + place
-                    y = lax.rem(owner - z + 2 * NZ, NY)
+            for place in range(2):
+                for y in range(NY):
                     for core in range(2):
-                        at = ((owner * 2 + place) * 2 + core) * CAP
-                        part[core, z, y] = rows[at : at + CAP].astype(BF16)
+                        at = ((place * NY + y) * 2 + core) * CAP
+                        part[core, 2 * pair + place, y] = rows[at : at + CAP].astype(BF16)
             both = pl.ds(2 * pair, 2)
             self.copies.append(net.send(part.at[net.o, both], other.at[both], net.twin))
             if k:
@@ -288,7 +304,7 @@
     count_ref, pos_ref, res_ref, cot_ref, rw_ref, win_ref, wout_ref,
     fin_out, sel_out,
     send_sem, recv_sem, load_sem, winp, woutp, counts, contrib, from_twin, from_mate, g0, g1,
-    pr, prl, pd, pdl, proj, dj, kv, joined, dproj, kg, kgl,
+    pr, prl, pd, pdl, proj, dj, qkv, joined, datt, dproj, qn, kn, dkey_n, dvalues,
     delta, dnormed, stats, fin, *bufs,
 ):
     net = Net(send_sem, recv_sem)
@@ -492,81 +508,60 @@
     logit = jnp.sum(jnp.where((lane >= at + 3) & (lane < at + 6), tail, 0.0), axis=-1, keepdims=True)
     in_scale = lax.rsqrt(square / D + 1e-05)
     gate = jax.nn.sigmoid(logit)
-    keyraw = proj[:, :, HS : 2 * HS].reshape(BLK, HS) * in_scale
-    key_scale = lax.rsqrt(jnp.mean(keyraw * keyraw, axis=-1, keepdims=True) + 1e-06)
-    kv[x, :, 0:HS] = (keyraw * key_scale).astype(BF16)
-    kv[x, :, HS : 2 * HS] = (proj[:, :, 2 * HS : 3 * HS].reshape(BLK, HS) * in_scale).astype(BF16)
-    kv_gather = MpGather(net, kv, slice(0, 2 * HS))
+    give(net, qkv, slice(0, 3 * HS), (proj[:, :, 0 : 3 * HS].reshape(BLK, 3 * HS) * in_scale).astype(BF16))
+    qkv_gather = MpGather(net, qkv, slice(0, 3 * HS))
 
     gate_up = proj[:, :, 384:896].reshape(BLK, 512) * in_scale
     gate_in = gate_up[:, 0:FFD]
     up_in = gate_up[:, FFD : 2 * FFD]
     sigma = jax.nn.sigmoid(gate_in)
-    joined[x, :, 256:384] = jnp.zeros((BLK, 128), BF16)
-    joined[x, :, HS : HS + FFD] = (gate_in * sigma * up_in).astype(BF16)
+    hidden = (gate_in * sigma * up_in).astype(BF16)
+    give(net, joined, slice(HS, WOUTP), jnp.concatenate([hidden, jnp.zeros((BLK, 32), BF16)], axis=-1))
     hid_ring = MpRing(net, joined, slice(HS, WOUTP))
-
     arrive(*d_2)
     back_2 = back_stage(2, -2)
     arrive(*d_3)
     back_3 = back_stage(3, -3)
     arrive(*d_4)
     back_4 = back_stage(4)
-    query = proj[:, :, 0:HS].reshape(BLK, HS) * in_scale
+    qkv_gather.done()
+
+    query = qkv[:, :, :, 0:HS].reshape(ROWS, HS).astype(F32)
+    keyraw = qkv[:, :, :, HS : 2 * HS].reshape(ROWS, HS).astype(F32)
+    vals = qkv[:, :, :, 2 * HS : 3 * HS].reshape(ROWS, HS)
     query_scale = lax.rsqrt(jnp.mean(query * query, axis=-1, keepdims=True) + 1e-06)
-    query_b = (query * query_scale).astype(BF16)
-    row = lax.broadcasted_iota(jnp.int32, (BLK, 1), 0)
-    row_z = row >> 5
-    query_order = row_z * 128 + ((x + 8 - row_z) & 3) * 32 + (row & 31)
-    col = lax.broadcasted_iota(jnp.int32, (1, ROWS), 1)
-    col_z = (col >> 5) & 7
-    key_order = col_z * 128 + (((col >> 8) + 8 - col_z) & 3) * 32 + (col & 31)
-    visible = key_order <= query_order
-    kv_gather.done()
-
-    keys = kv[:, :, 0:HS].reshape(ROWS, HS)
-    vals = kv[:, :, HS : 2 * HS].reshape(ROWS, HS)
-    expo = jnp.where(visible, jnp.exp(dot_nt(query_b, keys) * FACTOR), 0.0)
-    inverse = 1.0 / jnp.sum(expo, axis=-1, keepdims=True)
-    joined[x, :, 0:HS] = (dot_nn(expo.astype(BF16), vals) * inverse).astype(BF16)
-    att_gather = MpGather(net, joined, slice(0, HS))
+    key_scale = lax.rsqrt(jnp.mean(keyraw * keyraw, axis=-1, keepdims=True) + 1e-06)
+    qn[...] = (query * query_scale).astype(BF16)
+    kn[...] = (keyraw * key_scale).astype(BF16)
+
+    def exp_scores(block):
+        first, last = block * BLK, block * BLK + BLK
+        raw = dot_nt(qn[first:last], kn[0:last])
+        row = lax.broadcasted_iota(jnp.int32, (BLK, 1), 0) + first
+        visible = lax.broadcasted_iota(jnp.int32, (1, last), 1) <= row
+        return jnp.where(visible, jnp.exp(raw * FACTOR), 0.0)
+
+    inverse = []
+    for block in range(4):
+        expo = exp_scores(block)
+        inverse.append(1.0 / jnp.sum(expo, axis=-1, keepdims=True))
+        attended = dot_nn(expo.astype(BF16), vals[0 : block * BLK + BLK]) * inverse[block]
+        joined[2 * block : 2 * block + 2, :, :, 0:HS] = attended.astype(BF16).reshape(2, NY, 32, HS)
+    hid_ring.pass_on()
 
     for items in (back_0, back_1, back_2, back_3, back_4):
         collect(dj, items)
-    dattended = (dj[:, :, 0:HS].reshape(BLK, HS) * gate).astype(BF16)
+    give(net, datt, slice(0, HS), (dj[:, :, 0:HS].reshape(BLK, HS) * gate).astype(BF16))
+    datt_gather = MpGather(net, datt, slice(0, HS))
     dhidden = dj[:, :, HS:WOUTP].reshape(BLK, 256)[:, 0:FFD] * gate
     dup = (dhidden * gate_in * sigma).astype(BF16)
     dgate_in = (dhidden * up_in * sigma * (1.0 + gate_in * (1.0 - sigma))).astype(BF16)
-    dproj[x, :, 384:896] = jnp.concatenate([dgate_in, dup, jnp.zeros((BLK, 64), BF16)], axis=-1)
-
-    prob = expo * inverse
-    dprob = dot_nt(dattended, vals)
-    inner = jnp.sum(prob * dprob, axis=-1, keepdims=True)
-    dscore = (prob * (dprob - inner)).astype(BF16)
-    prob_b = prob.astype(BF16)
-    dkey_part = (dot_tn(dscore, query_b) * FACTOR).astype(BF16)
-    dvalue_part = dot_tn(prob_b, dattended).astype(BF16)
-    for owner in range(NX):
-        kg[owner, :, 0:HS] = dkey_part[owner * BLK : owner * BLK + BLK]
-        kg[owner, :, HS : 2 * HS] = dvalue_part[owner * BLK : owner * BLK + BLK]
-    kg_sum = MpSum(net, kg, kgl)
-    hid_ring.pass_on()
+    give(net, dproj, slice(384, 896), jnp.concatenate([dgate_in, dup, jnp.zeros((BLK, 64), BF16)], axis=-1))
     ff_ring = MpRing(net, dproj, slice(384, WINP))
-    dquery_n = dot_nn(dscore, keys) * FACTOR
-
-    def norm_back(values, scale, grads):
-        return scale * grads - values * scale**3 * jnp.mean(grads * values, axis=-1, keepdims=True)
-
-    dproj[x, :, 0:HS] = norm_back(query, query_scale, dquery_n).astype(BF16)
-    key_grad = kg_sum.total()
-    dproj[x, :, HS : 2 * HS] = norm_back(keyraw, key_scale, key_grad[:, 0:HS]).astype(BF16)
-    dproj[x, :, 2 * HS : 3 * HS] = key_grad[:, HS : 2 * HS].astype(BF16)
-    qkv_gather = MpGather(net, dproj, slice(0, 3 * HS))
-    att_gather.done()
     hid_ring.done()
 
     def rows_of(full, pair, columns):
-        return full[:, pl.ds(pl.multiple_of(pair * 64, 64), 64)].reshape(BLK, columns)
+        return full[pl.ds(2 * pair, 2)].reshape(BLK, columns)
 
     pair = lax.div(z, 2)
     turned = 1 - 2 * lax.rem(z, 2)
@@ -578,12 +573,36 @@
     dnormed_sum = SeqSum(
         net, bufs[n_bufs:], dnormed, lambda pair: dot_nn(rows_of(dproj, pair, WINP), winp[...]), far_first
     )
+    delta_sum.multiply(False)
     ff_ring.pass_on()
-    delta_sum.multiply(False)
+    datt_gather.done()
+
+    def norm_back(values, scale, grads):
+        return scale * grads - values * scale**3 * jnp.mean(grads * values, axis=-1, keepdims=True)
+
+    for block in range(3, -1, -1):
+        first, last = block * BLK, block * BLK + BLK
+        prob = exp_scores(block) * inverse[block]
+        dout = datt[2 * block : 2 * block + 2].reshape(BLK, HS)
+        dprob = dot_nt(dout, vals[0:last])
+        inner = jnp.sum(prob * dprob, axis=-1, keepdims=True)
+        dscore = (prob * (dprob - inner)).astype(BF16)
+        dquery_n = dot_nn(dscore, kn[0:last]) * FACTOR
+        dquery = norm_back(query[first:last], query_scale[first:last], dquery_n)
+        dproj[2 * block : 2 * block + 2, :, :, 0:HS] = dquery.astype(BF16).reshape(2, NY, 32, HS)
+        dkey_part = dot_tn(dscore, qn[first:last])
+        dvalue_part = dot_tn(prob.astype(BF16), dout)
+        if block == 3:
+            dkey_n[...] = dkey_part
+            dvalues[...] = dvalue_part
+        else:
+            dkey_n[0:last] = dkey_n[0:last] + dkey_part
+            dvalues[0:last] = dvalues[0:last] + dvalue_part
+    dkey = norm_back(keyraw, key_scale, dkey_n[...] * FACTOR)
+    dproj[:, :, :, HS : 2 * HS] = dkey.astype(BF16).reshape(NZ, NY, 32, HS)
+    dproj[:, :, :, 2 * HS : 3 * HS] = dvalues[...].astype(BF16).reshape(NZ, NY, 32, HS)
     delta_sum.turn()
     ff_ring.done()
-    qkv_gather.done()
-    delta_sum.turn()
     dnormed_sum.multiply(True)
     while delta_sum.turn():
         dnormed_sum.turn()
@@ -655,7 +674,7 @@
 
 
 def local(residual, chosen_pos, chosen_count, router_weight, weight_in, weight_out, cotangent):
-    n_sem = 109
+    n_sem = 107
     scratch = [
         pltpu.SemaphoreType.DMA((n_sem,)),
         pltpu.SemaphoreType.DMA((n_sem,)),
@@ -674,11 +693,14 @@
         pltpu.VMEM((NZ, NX - 1, 32, WOUTP), BF16),
         pltpu.VMEM((NZ, 32, WINP), F32),
         pltpu.VMEM((NZ, 32, WOUTP), F32),
-        pltpu.VMEM((NX, BLK, 2 * HS), BF16),
-        pltpu.VMEM((NX, BLK, WOUTP), BF16),
-        pltpu.VMEM((NX, BLK, WINP), BF16),
-        pltpu.VMEM((NX, BLK, 2 * HS), BF16),
-        pltpu.VMEM((NX - 1, BLK, 2 * HS), BF16),
+        pltpu.VMEM((NZ, NY, 32, 3 * HS), BF16),
+        pltpu.VMEM((NZ, NY, 32, WOUTP), BF16),
+        pltpu.VMEM((NZ, NY, 32, HS), BF16),
+        pltpu.VMEM((NZ, NY, 32, WINP), BF16),
+        pltpu.VMEM((ROWS, HS), BF16),
+        pltpu.VMEM((ROWS, HS), BF16),
+        pltpu.VMEM((ROWS, HS), F32),
+        pltpu.VMEM((ROWS, HS), F32),
         pltpu.VMEM((CAP, QD), F32),
         pltpu.VMEM((CAP, QD), F32),
         pltpu.VMEM((3, 4, CAP, 128), F32),

time: 171 us -> 148 us (0.87)
  Pallas kernels: 170 us -> 147 us
    pallas_call x1, Pallas kernels: 167 us -> 144 us  [local(): pl.pallas_call(kernel, out_shape=[jax.ShapeDtypeStruct((2, 4, CAP, QD), B...]
where the time goes in v4:
time: 148 us
  Pallas kernels  147 us (99%)
    pallas_call x1, Pallas kernels, local(): pl.pallas_call(kernel, out_shape=[jax.ShapeDtypeStruct((2, 4, CAP, QD), B...  144 us

profile of v4, /device:TPU:1, one launch (start us, length us, event | category | flops | bytes accessed | tf_op | source)
XLA Modules:
  0.0 147.9 jit_solution(10269979833114970266)
XLA Ops:
  1.3 143.9 %shard_map.86 = (bf16[2,4,16,2048]{3,2,1,0:T(8,128)(2,1)}, bf16[64,128]{1,0:T(8,128)(2,1)}) custom-call(s32[1,1]{1,0:T(1,128)} %bitcast.5.count_ref, s32[1,48]{1,0:T(1,128)} %bitcast.9, bf16[128,2048]{1,0:T(8,128)(2,1)} %res_ref.3, bf16[128,2048]{1,0:T(8,128)(2,1)} %cot_ref.3, f32[1,2048]{1,0:T(1,128)} %bitcast.8, bf16[832,2048]{1,0:T(8,128)(2,1)} %bitcast.7, ...), custom_call_target="tpu_custom_call" | custom-call | flops 10000000000 | bytes 10000000 | tf_op jit(solution)/shard_map/pallas_call | solution.py:711
  145.2 2.7 %shard_map.87 = (bf16[128,2048]{1,0:T(8,128)(2,1)}, bf16[128,2048]{1,0:T(8,128)(2,1)}) custom-call(bf16[64,128]{1,0:T(8,128)(2,1)} %get-tuple-element.4.sel_ref, bf16[2,64,2048]{2,1,0:T(8,128)(2,1)} %bitcast.6, bf16[128,2048]{1,0:T(8,128)(2,1)} %res_ref.3, bf16[128,2048]{1,0:T(8,128)(2,1)} %cot_ref.3), custom_call_target="tpu_custom_call" | custom-call | tf_op jit(solution)/shard_map/pallas_call | solution.py:733

commit v5 on v4

--- a/solution.py
+++ b/solution.py
@@ -19,8 +19,11 @@
 ROWS = 1024
 BLK = 256
 HALF = QD // 2
-Z_FIRST = ((0, 512), (512, 256))
-AW = 768
+AW = 512
+BW = QD - AW
+MIX = 2 * WOUTP
+HID = 3 * HS
+ATT = HID + 256
 F32 = jnp.float32
 BF16 = jnp.bfloat16
 FACTOR = HS ** (-0.5)
@@ -88,6 +91,24 @@
         self.sent.append(pltpu.make_async_copy(whole, whole, send_sem))
         return pltpu.make_async_copy(whole, whole, recv_sem)
 
+    def open(self):
+        self.used += 1
+        return self.used - 1
+
+    def put(self, which, src, dst, device):
+        pltpu.make_async_remote_copy(
+            src_ref=src,
+            dst_ref=dst,
+            send_sem=self.send_sem.at[which],
+            recv_sem=self.recv_sem.at[which],
+            device_id=device,
+            device_id_type=MESH,
+        ).start()
+
+    def close(self, which, whole):
+        self.sent.append(pltpu.make_async_copy(whole, whole, self.send_sem.at[which]))
+        return pltpu.make_async_copy(whole, whole, self.recv_sem.at[which])
+
     def send(self, src, dst, device):
         return self.group([(src, dst, device)], dst)
 
@@ -164,132 +185,94 @@
         arrive(self.copy)
 
 
-def chain(net, pos, block, from_left, from_right, width):
-    hops = NZ // 2
-    half = width // 2
-    far = mod(pos + hops, NZ)
-    copy = net.group(
-        [
-            (block(far, 0, half), from_left.at[0, ..., 0:half], net.zp),
-            (block(far, half, width), from_right.at[0, ..., half:width], net.zm),
-        ],
-        from_left.at[0],
-    )
-    yield
-    for step in range(1, hops):
-        right, left = mod(pos + hops - step, NZ), mod(pos - hops + step, NZ)
-        arrive(copy)
-        for at, landed, (lo, hi) in ((right, from_left, (0, half)), (left, from_right, (half, width))):
-            if step > 1:
-                lo, hi = 0, width
-            target = block(at, lo, hi)
-            target[...] = (target[...].astype(F32) + landed[step - 1, ..., lo:hi].astype(F32)).astype(BF16)
-        copy = net.group(
-            [
-                (block(right, 0, width), from_left.at[step], net.zp),
-                (block(left, 0, width), from_right.at[step], net.zm),
-            ],
-            from_left.at[0:2],
-        )
-        yield
-    arrive(copy)
-
-
 class SeqSum:
     def __init__(self, net, bufs, out, product, order):
-        self.net, self.bufs, self.out, self.product, self.order = net, bufs, out, product, order
-        self.by_copies, self.by_all = [], []
-        self.steps = [self.along_z_first(0), self.along_z_first(1)]
+        self.net, self.out, self.product, self.order = net, out, product, order
+        self.part, self.other, self.qa, self.qb, self.azl, self.ayl, self.byl, self.bzl = bufs
+        self.along_z_a, self.along_z_b = net.open(), net.open()
+        self.along_y_b = []
+        self.finished = 0
+        self.steps = self.finish()
+
+    def places(self, k):
+        pair = self.order[k]
+        both = (2 * pair, 2 * pair + 1)
+        return both, both if k < 3 else (2 * pair + 1 - lax.rem(self.net.z, 2),)
+
+    def at_z(self, z):
+        return self.net.at(z, self.net.y, self.net.c, self.net.x)
 
     def multiply(self, eager):
-        net, part, other = self.net, self.bufs[0], self.bufs[1]
-        self.copies = []
+        net, copies = self.net, []
         for k, pair in enumerate(self.order):
             rows = self.product(pair)
             for place in range(2):
                 for y in range(NY):
                     for core in range(2):
                         at = ((place * NY + y) * 2 + core) * CAP
-                        part[core, 2 * pair + place, y] = rows[at : at + CAP].astype(BF16)
+                        self.part[core, 2 * pair + place, y] = rows[at : at + CAP].astype(BF16)
             both = pl.ds(2 * pair, 2)
-            self.copies.append(net.send(part.at[net.o, both], other.at[both], net.twin))
+            copies.append(net.send(self.part.at[net.o, both], self.other.at[both], net.twin))
             if k:
-                self.merge(k - 1)
+                self.merge(k - 1, copies[k - 1])
             if k == 3 and eager:
-                self.turn()
-        self.merge(len(self.order) - 1)
-        self.steps.append(self.along_y_first())
-
-    def merge(self, k):
-        net, part, other, byl = self.net, self.bufs[0], self.bufs[1], self.bufs[9]
-        arrive(self.copies[k])
-        pair = self.order[k]
-        for place in range(2):
-            z = 2 * pair + place
-            part[net.c, z] = (part[net.c, z].astype(F32) + other[z].astype(F32)).astype(BF16)
-        if k == 0:
-            for step in self.steps:
-                next(step)
-        both = pl.ds(2 * pair, 2)
-        for d in range(1, NY):
-            source = part.at[net.c, both, mod(net.y + d, NY), :, AW:QD]
-            self.by_copies.append((source, byl.at[d - 1, both], net.along_y[d - 1]))
-        self.by = net.group(self.by_copies, byl.at[:, 0:2])
-        self.by_copies = []
-        self.by_all.append(self.by)
+                self.sum_y(0)
+        self.merge(3, copies[3])
+
+    def merge(self, k, copy):
+        net, part = self.net, self.part
+        arrive(copy)
+        both, others = self.places(k)
+        for z in both:
+            part[net.c, z] = (part[net.c, z].astype(F32) + self.other[z].astype(F32)).astype(BF16)
+        for z in others:
+            net.put(self.along_z_a, part.at[net.c, z, :, :, 0:AW], self.azl.at[net.z], self.at_z(z))
+        rows = pl.ds(2 * self.order[k], 2)
+        copies = [
+            (part.at[net.c, rows, mod(net.y + d, NY), :, AW:QD], self.byl.at[d - 1, rows], net.along_y[d - 1])
+            for d in range(1, NY)
+        ]
+        self.along_y_b.append(net.group(copies, self.byl.at[:, 0:2]))
+
+    def sum_y(self, k):
+        net = self.net
+        arrive(self.along_y_b[k])
+        both, others = self.places(k)
+        for z in both:
+            total = self.part[net.c, z, net.y, :, AW:QD].astype(F32)
+            for d in range(NY - 1):
+                total = total + self.byl[d, z].astype(F32)
+            self.qb[z] = total.astype(BF16)
+        for z in others:
+            net.put(self.along_z_b, self.qb.at[z], self.bzl.at[net.z], self.at_z(z))
+        self.finished = k + 1
 
     def turn(self):
-        left = []
-        for step in self.steps:
-            try:
-                next(step)
-                left.append(step)
-            except StopIteration:
-                pass
-        self.steps = left
-        return bool(left)
-
-    def along_z_first(self, which):
-        net, part, qa, ayl = self.net, self.bufs[0], self.bufs[2], self.bufs[8]
-        first, width = Z_FIRST[which]
-        left, right = self.bufs[4 + 2 * which], self.bufs[5 + 2 * which]
-        block = lambda t, lo, hi: part.at[net.c, t, :, :, first + lo : first + hi]
-        yield from chain(net, net.z, block, left, right, width)
-        last = NZ // 2 - 1
-        lanes = slice(first, first + width)
-        qa[:, :, lanes] = (
-            part[net.c, net.z, :, :, lanes].astype(F32) + left[last].astype(F32) + right[last].astype(F32)
-        ).astype(BF16)
+        return next(self.steps, None) is not None
+
+    def finish(self):
+        net = self.net
+        for k in range(self.finished, 4):
+            self.sum_y(k)
+        arrive(net.close(self.along_z_a, self.azl.at[0 : NZ - 1]))
+        total = self.part[net.c, net.z, :, :, 0:AW].astype(F32)
+        for d in range(1, NZ):
+            total = total + self.azl[mod(net.z + d, NZ)].astype(F32)
+        self.qa[...] = total.astype(BF16)
         copy = net.group(
-            [
-                (qa.at[mod(net.y + d, NY), :, lanes], ayl.at[d - 1, :, lanes], net.along_y[d - 1])
-                for d in range(1, NY)
-            ],
-            ayl.at[:, :, lanes],
+            [(self.qa.at[mod(net.y + d, NY)], self.ayl.at[d - 1], net.along_y[d - 1]) for d in range(1, NY)], self.ayl
         )
-        yield
+        yield True
+        arrive(net.close(self.along_z_b, self.bzl.at[0 : NZ - 1]))
+        total = self.qb[net.z].astype(F32)
+        for d in range(1, NZ):
+            total = total + self.bzl[mod(net.z + d, NZ)].astype(F32)
+        self.out[:, AW:QD] = total
         arrive(copy)
-        total = qa[net.y, :, lanes].astype(F32)
+        total = self.qa[net.y].astype(F32)
         for d in range(NY - 1):
-            total = total + ayl[d, :, lanes].astype(F32)
-        self.out[:, lanes] = total
-
-    def along_y_first(self):
-        net, part, qb, byl, bzl = self.net, self.bufs[0], self.bufs[3], self.bufs[9], self.bufs[10]
-        arrive(*self.by_all)
-        total = part[net.c, :, net.y, :, AW:QD].astype(F32)
-        for d in range(NY - 1):
-            total = total + byl[d].astype(F32)
-        qb[...] = total.astype(BF16)
-        copy = net.group(
-            [(qb.at[mod(net.z + d, NZ)], bzl.at[d - 1], net.along_z[d - 1]) for d in range(1, NZ)], bzl
-        )
-        yield
-        arrive(copy)
-        total = qb[net.z].astype(F32)
-        for d in range(NZ - 1):
-            total = total + bzl[d].astype(F32)
-        self.out[:, AW:QD] = total
+            total = total + self.ayl[d].astype(F32)
+        self.out[:, 0:AW] = total
 
 
 def row_sums(tile, columns):
@@ -304,14 +287,15 @@
     count_ref, pos_ref, res_ref, cot_ref, rw_ref, win_ref, wout_ref,
     fin_out, sel_out,
     send_sem, recv_sem, load_sem, winp, woutp, counts, contrib, from_twin, from_mate, g0, g1,
-    pr, prl, pd, pdl, proj, dj, qkv, joined, datt, dproj, qn, kn, dkey_n, dvalues,
+    pr, prl, pd, pdl, proj, dj, mixed, datt, dproj, qn, kn, dkey_n, dvalues,
     delta, dnormed, stats, fin, *bufs,
 ):
     net = Net(send_sem, recv_sem)
     x, y, z, c = net.x, net.y, net.z, net.c
     loads = (
         pltpu.make_async_copy(win_ref, winp.at[0:WIN], load_sem.at[0]),
-        pltpu.make_async_copy(wout_ref, woutp.at[0:WOUT], load_sem.at[1]),
+        pltpu.make_async_copy(wout_ref.at[HS:WOUT], woutp.at[0:FFD], load_sem.at[1]),
+        pltpu.make_async_copy(wout_ref.at[0:HS], woutp.at[256:WOUTP], load_sem.at[2]),
     )
     for load in loads:
         load.start()
@@ -426,6 +410,32 @@
         for at, part in items:
             target[at] = part.total()
 
+    def add_up(value, first, last):
+        lanes = lane[0 : value.shape[0]]
+        return jnp.sum(jnp.where((lanes >= first) & (lanes < last), value, 0.0), axis=-1, keepdims=True)
+
+    def scale_of(tail):
+        at = WIN - 768
+        return lax.rsqrt(add_up(tail, at, at + 3) / D + 1e-05)
+
+    def project(items):
+        copies = []
+        for at, part in items:
+            total = part.total()
+            proj[at] = total
+            scale = scale_of(total[:, 768:896])
+            row = lax.rem(x - at + NZ, NX)
+            gate_up = total[:, 384:896] * scale
+            gate_in = gate_up[:, 0:FFD]
+            hidden = (gate_in * jax.nn.sigmoid(gate_in) * gate_up[:, FFD : 2 * FFD]).astype(BF16)
+            mixed[at, row, :, 0:HID] = (total[:, 0:HID] * scale).astype(BF16)
+            mixed[at, row, :, HID:ATT] = jnp.concatenate([hidden, jnp.zeros((32, 256 - FFD), BF16)], axis=-1)
+            block = mixed.at[at, row, :, 0:ATT]
+            copies.append(
+                net.group([(block, block, device) for device in net.along_x], mixed.at[at, 0 : NX - 1, :, 0:ATT])
+            )
+        return copies
+
     other_q = 1 - mine_q
     p_ring = r_ring(1, mine_q)
     r_copy = net.same(g0.at[z, pl.ds(2 * mine_q, 2), c], net.beyond)
@@ -443,7 +453,7 @@
 
     first_stats = stats_out(0)
     winp[WIN:WINP] = jnp.zeros((WINP - WIN, QD), BF16)
-    woutp[WOUT:WOUTP] = jnp.zeros((WOUTP - WOUT, QD), BF16)
+    woutp[FFD:256] = jnp.zeros((256 - FFD, QD), BF16)
     for load in loads:
         load.wait()
     arrive(r_copy)
@@ -490,45 +500,35 @@
     in_3 = in_stage(3, -3)
     arrive(p_ring, q_ring)
     r_4 = r_twin(4)
-    collect(proj, in_0)
-    collect(proj, in_1)
+    mixed_rows = project(in_0) + project(in_1)
     arrive(*r_4)
     in_4 = in_stage(4)
     arrive(*d_1)
     back_1 = back_stage(1, -1)
     d_3 = d_twin(d_3)
-    collect(proj, in_2)
-    collect(proj, in_3)
+    mixed_rows += project(in_2)
+    mixed_rows += project(in_3)
+    arrive(*d_2)
+    back_2 = back_stage(2, -2)
     d_4 = d_twin(d_4)
-    collect(proj, in_4)
-
+    mixed_rows += project(in_4)
+
+    arrive(*d_3)
+    back_3 = back_stage(3, -3)
+    arrive(*d_4)
+    back_4 = back_stage(4)
     tail = proj[:, :, 768:896].reshape(BLK, 128)
-    at = WIN - 768
-    square = jnp.sum(jnp.where((lane >= at) & (lane < at + 3), tail, 0.0), axis=-1, keepdims=True)
-    logit = jnp.sum(jnp.where((lane >= at + 3) & (lane < at + 6), tail, 0.0), axis=-1, keepdims=True)
-    in_scale = lax.rsqrt(square / D + 1e-05)
-    gate = jax.nn.sigmoid(logit)
-    give(net, qkv, slice(0, 3 * HS), (proj[:, :, 0 : 3 * HS].reshape(BLK, 3 * HS) * in_scale).astype(BF16))
-    qkv_gather = MpGather(net, qkv, slice(0, 3 * HS))
-
+    in_scale = scale_of(tail)
+    gate = jax.nn.sigmoid(add_up(tail, WIN - 765, WIN - 762))
     gate_up = proj[:, :, 384:896].reshape(BLK, 512) * in_scale
     gate_in = gate_up[:, 0:FFD]
     up_in = gate_up[:, FFD : 2 * FFD]
     sigma = jax.nn.sigmoid(gate_in)
-    hidden = (gate_in * sigma * up_in).astype(BF16)
-    give(net, joined, slice(HS, WOUTP), jnp.concatenate([hidden, jnp.zeros((BLK, 32), BF16)], axis=-1))
-    hid_ring = MpRing(net, joined, slice(HS, WOUTP))
-    arrive(*d_2)
-    back_2 = back_stage(2, -2)
-    arrive(*d_3)
-    back_3 = back_stage(3, -3)
-    arrive(*d_4)
-    back_4 = back_stage(4)
-    qkv_gather.done()
-
-    query = qkv[:, :, :, 0:HS].reshape(ROWS, HS).astype(F32)
-    keyraw = qkv[:, :, :, HS : 2 * HS].reshape(ROWS, HS).astype(F32)
-    vals = qkv[:, :, :, 2 * HS : 3 * HS].reshape(ROWS, HS)
+    arrive(*mixed_rows)
+
+    query = mixed[:, :, :, 0:HS].reshape(ROWS, HS).astype(F32)
+    keyraw = mixed[:, :, :, HS : 2 * HS].reshape(ROWS, HS).astype(F32)
+    vals = mixed[:, :, :, 2 * HS : 3 * HS].reshape(ROWS, HS)
     query_scale = lax.rsqrt(jnp.mean(query * query, axis=-1, keepdims=True) + 1e-06)
     key_scale = lax.rsqrt(jnp.mean(keyraw * keyraw, axis=-1, keepdims=True) + 1e-06)
     qn[...] = (query * query_scale).astype(BF16)
@@ -546,32 +546,31 @@
         expo = exp_scores(block)
         inverse.append(1.0 / jnp.sum(expo, axis=-1, keepdims=True))
         attended = dot_nn(expo.astype(BF16), vals[0 : block * BLK + BLK]) * inverse[block]
-        joined[2 * block : 2 * block + 2, :, :, 0:HS] = attended.astype(BF16).reshape(2, NY, 32, HS)
-    hid_ring.pass_on()
+        mixed[2 * block : 2 * block + 2, :, :, ATT:MIX] = attended.astype(BF16).reshape(2, NY, 32, HS)
 
     for items in (back_0, back_1, back_2, back_3, back_4):
         collect(dj, items)
-    give(net, datt, slice(0, HS), (dj[:, :, 0:HS].reshape(BLK, HS) * gate).astype(BF16))
+    give(net, datt, slice(0, HS), (dj[:, :, 256:WOUTP].reshape(BLK, HS) * gate).astype(BF16))
     datt_gather = MpGather(net, datt, slice(0, HS))
-    dhidden = dj[:, :, HS:WOUTP].reshape(BLK, 256)[:, 0:FFD] * gate
+    dhidden = dj[:, :, 0:256].reshape(BLK, 256)[:, 0:FFD] * gate
     dup = (dhidden * gate_in * sigma).astype(BF16)
     dgate_in = (dhidden * up_in * sigma * (1.0 + gate_in * (1.0 - sigma))).astype(BF16)
     give(net, dproj, slice(384, 896), jnp.concatenate([dgate_in, dup, jnp.zeros((BLK, 64), BF16)], axis=-1))
     ff_ring = MpRing(net, dproj, slice(384, WINP))
-    hid_ring.done()
-
-    def rows_of(full, pair, columns):
-        return full[pl.ds(2 * pair, 2)].reshape(BLK, columns)
+
+    def rows_of(full, pair, lanes):
+        rows = full[pl.ds(2 * pair, 2), :, :, lanes]
+        return rows.reshape(BLK, rows.shape[-1])
 
     pair = lax.div(z, 2)
     turned = 1 - 2 * lax.rem(z, 2)
     far_first = (mod(pair + 2, 4), mod(pair + turned, 4), mod(pair - turned, 4), pair)
     n_bufs = len(bufs) // 2
     delta_sum = SeqSum(
-        net, bufs[:n_bufs], delta, lambda pair: dot_nn(rows_of(joined, pair, WOUTP), woutp[...]), far_first
+        net, bufs[:n_bufs], delta, lambda pair: dot_nn(rows_of(mixed, pair, slice(HID, MIX)), woutp[...]), far_first
     )
     dnormed_sum = SeqSum(
-        net, bufs[n_bufs:], dnormed, lambda pair: dot_nn(rows_of(dproj, pair, WINP), winp[...]), far_first
+        net, bufs[n_bufs:], dnormed, lambda pair: dot_nn(rows_of(dproj, pair, slice(0, WINP)), winp[...]), far_first
     )
     delta_sum.multiply(False)
     ff_ring.pass_on()
@@ -662,23 +661,20 @@
         pltpu.VMEM((2, NZ, NY, CAP, QD), BF16),
         pltpu.VMEM((NZ, NY, CAP, QD), BF16),
         pltpu.VMEM((NY, CAP, AW), BF16),
-        pltpu.VMEM((NZ, CAP, QD - AW), BF16),
-        pltpu.VMEM((NZ // 2, NY, CAP, Z_FIRST[0][1]), BF16),
-        pltpu.VMEM((NZ // 2, NY, CAP, Z_FIRST[0][1]), BF16),
-        pltpu.VMEM((NZ // 2, NY, CAP, Z_FIRST[1][1]), BF16),
-        pltpu.VMEM((NZ // 2, NY, CAP, Z_FIRST[1][1]), BF16),
+        pltpu.VMEM((NZ, CAP, BW), BF16),
+        pltpu.VMEM((NZ, NY, CAP, AW), BF16),
         pltpu.VMEM((NY - 1, CAP, AW), BF16),
-        pltpu.VMEM((NY - 1, NZ, CAP, QD - AW), BF16),
-        pltpu.VMEM((NZ - 1, CAP, QD - AW), BF16),
+        pltpu.VMEM((NY - 1, NZ, CAP, BW), BF16),
+        pltpu.VMEM((NZ, CAP, BW), BF16),
     ]
 
 
 def local(residual, chosen_pos, chosen_count, router_weight, weight_in, weight_out, cotangent):
-    n_sem = 107
+    n_sem = 96
     scratch = [
         pltpu.SemaphoreType.DMA((n_sem,)),
         pltpu.SemaphoreType.DMA((n_sem,)),
-        pltpu.SemaphoreType.DMA((2,)),
+        pltpu.SemaphoreType.DMA((3,)),
         pltpu.VMEM((WINP, QD), BF16),
         pltpu.VMEM((WOUTP, QD), BF16),
         pltpu.VMEM((2, 8, 128), jnp.int32),
@@ -693,8 +689,7 @@
         pltpu.VMEM((NZ, NX - 1, 32, WOUTP), BF16),
         pltpu.VMEM((NZ, 32, WINP), F32),
         pltpu.VMEM((NZ, 32, WOUTP), F32),
-        pltpu.VMEM((NZ, NY, 32, 3 * HS), BF16),
-        pltpu.VMEM((NZ, NY, 32, WOUTP), BF16),
+        pltpu.VMEM((NZ, NY, 32, MIX), BF16),
         pltpu.VMEM((NZ, NY, 32, HS), BF16),
         pltpu.VMEM((NZ, NY, 32, WINP), BF16),
         pltpu.VMEM((ROWS, HS), BF16),

time: 148 us -> 140 us (0.946)
  Pallas kernels: 147 us -> 139 us
    pallas_call x1, Pallas kernels: 144 us -> 136 us  [local(): pl.pallas_call(kernel, out_shape=[jax.ShapeDtypeStruct((2, 4, CAP, QD), B...]
where the time goes in v5:
time: 140 us
  Pallas kernels  139 us (99%)
    pallas_call x1, Pallas kernels, local(): pl.pallas_call(kernel, out_shape=[jax.ShapeDtypeStruct((2, 4, CAP, QD), B...  136 us

profile of v5, /device:TPU:1, one launch (start us, length us, event | category | flops | bytes accessed | tf_op | source)
XLA Modules:
  0.0 140.2 jit_solution(14834516514295077095)
XLA Ops:
  1.3 136.2 %shard_map.86 = (bf16[2,4,16,2048]{3,2,1,0:T(8,128)(2,1)}, bf16[64,128]{1,0:T(8,128)(2,1)}) custom-call(s32[1,1]{1,0:T(1,128)} %bitcast.5.count_ref, s32[1,48]{1,0:T(1,128)} %bitcast.9, bf16[128,2048]{1,0:T(8,128)(2,1)} %res_ref.3, bf16[128,2048]{1,0:T(8,128)(2,1)} %cot_ref.3, f32[1,2048]{1,0:T(1,128)} %bitcast.8, bf16[832,2048]{1,0:T(8,128)(2,1)} %bitcast.7, ...), custom_call_target="tpu_custom_call" | custom-call | flops 10000000000 | bytes 10000000 | tf_op jit(solution)/shard_map/pallas_call | solution.py:706
  137.5 2.7 %shard_map.87 = (bf16[128,2048]{1,0:T(8,128)(2,1)}, bf16[128,2048]{1,0:T(8,128)(2,1)}) custom-call(bf16[64,128]{1,0:T(8,128)(2,1)} %get-tuple-element.4.sel_ref, bf16[2,64,2048]{2,1,0:T(8,128)(2,1)} %bitcast.6, bf16[128,2048]{1,0:T(8,128)(2,1)} %res_ref.3, bf16[128,2048]{1,0:T(8,128)(2,1)} %cot_ref.3), custom_call_target="tpu_custom_call" | custom-call | tf_op jit(solution)/shard_map/pallas_call | solution.py:728

commit v6 on v5

--- a/solution.py
+++ b/solution.py
@@ -188,10 +188,9 @@
 class SeqSum:
     def __init__(self, net, bufs, out, product, order):
         self.net, self.out, self.product, self.order = net, out, product, order
-        self.part, self.other, self.qa, self.qb, self.azl, self.ayl, self.byl, self.bzl = bufs
+        self.part, self.qa, self.qb, self.azl, self.ayl, self.byl, self.bzl = bufs
         self.along_z_a, self.along_z_b = net.open(), net.open()
         self.along_y_b = []
-        self.finished = 0
         self.steps = self.finish()
 
     def places(self, k):
@@ -202,34 +201,24 @@
     def at_z(self, z):
         return self.net.at(z, self.net.y, self.net.c, self.net.x)
 
-    def multiply(self, eager):
-        net, copies = self.net, []
-        for k, pair in enumerate(self.order):
-            rows = self.product(pair)
-            for place in range(2):
-                for y in range(NY):
-                    for core in range(2):
-                        at = ((place * NY + y) * 2 + core) * CAP
-                        self.part[core, 2 * pair + place, y] = rows[at : at + CAP].astype(BF16)
-            both = pl.ds(2 * pair, 2)
-            copies.append(net.send(self.part.at[net.o, both], self.other.at[both], net.twin))
-            if k:
-                self.merge(k - 1, copies[k - 1])
-            if k == 3 and eager:
-                self.sum_y(0)
-        self.merge(3, copies[3])
-
-    def merge(self, k, copy):
+    def multiply(self):
+        for half in range(2):
+            pairs = self.order[2 * half : 2 * half + 2]
+            rows = self.product(pairs)
+            for i, pair in enumerate(pairs):
+                for place in range(2):
+                    for y in range(NY):
+                        at = ((i * 2 + place) * NY + y) * CAP
+                        self.part[2 * pair + place, y] = rows[at : at + CAP].astype(BF16)
+                self.send(2 * half + i)
+
+    def send(self, k):
         net, part = self.net, self.part
-        arrive(copy)
-        both, others = self.places(k)
-        for z in both:
-            part[net.c, z] = (part[net.c, z].astype(F32) + self.other[z].astype(F32)).astype(BF16)
-        for z in others:
-            net.put(self.along_z_a, part.at[net.c, z, :, :, 0:AW], self.azl.at[net.z], self.at_z(z))
+        for z in self.places(k)[1]:
+            net.put(self.along_z_a, part.at[z, :, :, 0:AW], self.azl.at[net.z], self.at_z(z))
         rows = pl.ds(2 * self.order[k], 2)
         copies = [
-            (part.at[net.c, rows, mod(net.y + d, NY), :, AW:QD], self.byl.at[d - 1, rows], net.along_y[d - 1])
+            (part.at[rows, mod(net.y + d, NY), :, AW:QD], self.byl.at[d - 1, rows], net.along_y[d - 1])
             for d in range(1, NY)
         ]
         self.along_y_b.append(net.group(copies, self.byl.at[:, 0:2]))
@@ -239,23 +228,22 @@
         arrive(self.along_y_b[k])
         both, others = self.places(k)
         for z in both:
-            total = self.part[net.c, z, net.y, :, AW:QD].astype(F32)
+            total = self.part[z, net.y, :, AW:QD].astype(F32)
             for d in range(NY - 1):
                 total = total + self.byl[d, z].astype(F32)
             self.qb[z] = total.astype(BF16)
         for z in others:
             net.put(self.along_z_b, self.qb.at[z], self.bzl.at[net.z], self.at_z(z))
-        self.finished = k + 1
 
     def turn(self):
         return next(self.steps, None) is not None
 
     def finish(self):
         net = self.net
-        for k in range(self.finished, 4):
+        for k in range(4):
             self.sum_y(k)
         arrive(net.close(self.along_z_a, self.azl.at[0 : NZ - 1]))
-        total = self.part[net.c, net.z, :, :, 0:AW].astype(F32)
+        total = self.part[net.z, :, :, 0:AW].astype(F32)
         for d in range(1, NZ):
             total = total + self.azl[mod(net.z + d, NZ)].astype(F32)
         self.qa[...] = total.astype(BF16)
@@ -287,7 +275,7 @@
     count_ref, pos_ref, res_ref, cot_ref, rw_ref, win_ref, wout_ref,
     fin_out, sel_out,
     send_sem, recv_sem, load_sem, winp, woutp, counts, contrib, from_twin, from_mate, g0, g1,
-    pr, prl, pd, pdl, proj, dj, mixed, datt, dproj, qn, kn, dkey_n, dvalues,
+    pr, prl, pd, pdl, proj, dj, mixed, datt, dproj, winp2, woutp2, mixed2, dproj2, qn, kn, dkey_n, dvalues,
     delta, dnormed, stats, fin, *bufs,
 ):
     net = Net(send_sem, recv_sem)
@@ -436,6 +424,10 @@
             )
         return copies
 
+    def weights_out(quarter):
+        rows = slice(quarter * WINP // 4, (quarter + 1) * WINP // 4)
+        return net.send(winp.at[rows], winp2.at[rows], net.twin)
+
     other_q = 1 - mine_q
     p_ring = r_ring(1, mine_q)
     r_copy = net.same(g0.at[z, pl.ds(2 * mine_q, 2), c], net.beyond)
@@ -466,6 +458,7 @@
     p_ring = r_ring(2, mine_q)
     arrive(*r_0)
     in_0 = in_stage(0)
+    twin_weights = [net.send(woutp, woutp2, net.twin)]
     arrive(q_ring)
     q_ring = r_ring(2, other_q)
     r_1 = r_twin(1, -1)
@@ -477,6 +470,7 @@
     p_ring = r_ring(3, mine_q)
     arrive(*r_1)
     in_1 = in_stage(1, -1)
+    twin_weights.append(weights_out(0))
     arrive(q_ring)
     q_ring = r_ring(3, other_q)
     r_2 = r_twin(2, -2)
@@ -488,6 +482,7 @@
     p_ring = r_ring(4, mine_q)
     arrive(*r_2)
     in_2 = in_stage(2, -2)
+    twin_weights.append(weights_out(1))
     arrive(q_ring)
     q_ring = r_ring(4, other_q)
     r_3 = r_twin(3, -3)
@@ -498,11 +493,13 @@
     d_4 = d_out(4)
     arrive(*r_3)
     in_3 = in_stage(3, -3)
+    twin_weights.append(weights_out(2))
     arrive(p_ring, q_ring)
     r_4 = r_twin(4)
     mixed_rows = project(in_0) + project(in_1)
     arrive(*r_4)
     in_4 = in_stage(4)
+    twin_weights.append(weights_out(3))
     arrive(*d_1)
     back_1 = back_stage(1, -1)
     d_3 = d_twin(d_3)
@@ -547,6 +544,8 @@
         inverse.append(1.0 / jnp.sum(expo, axis=-1, keepdims=True))
         attended = dot_nn(expo.astype(BF16), vals[0 : block * BLK + BLK]) * inverse[block]
         mixed[2 * block : 2 * block + 2, :, :, ATT:MIX] = attended.astype(BF16).reshape(2, NY, 32, HS)
+    own_rows, twin_half = pl.multiple_of(c * CAP, CAP), pl.multiple_of(net.o * CAP, CAP)
+    mixed_copy = net.send(mixed.at[:, :, pl.ds(twin_half, CAP), HID:MIX], mixed2, net.twin)
 
     for items in (back_0, back_1, back_2, back_3, back_4):
         collect(dj, items)
@@ -558,21 +557,33 @@
     give(net, dproj, slice(384, 896), jnp.concatenate([dgate_in, dup, jnp.zeros((BLK, 64), BF16)], axis=-1))
     ff_ring = MpRing(net, dproj, slice(384, WINP))
 
-    def rows_of(full, pair, lanes):
-        rows = full[pl.ds(2 * pair, 2), :, :, lanes]
-        return rows.reshape(BLK, rows.shape[-1])
+    def rows_of(full, pairs, lanes, first):
+        rows = [full[pl.ds(2 * pair, 2), :, pl.ds(first, CAP), lanes] for pair in pairs]
+        return jnp.concatenate([part.reshape(BLK // 2, part.shape[-1]) for part in rows], axis=0)
+
+    def both_cores(full, lanes, weights, twin_rows, twin_weights, copies):
+        def product(pairs):
+            own = dot_nn(rows_of(full, pairs, lanes, own_rows), weights[...])
+            while copies:
+                arrive(copies.pop())
+            return own + dot_nn(rows_of(twin_rows, pairs, slice(0, twin_rows.shape[-1]), 0), twin_weights[...])
+
+        return product
 
     pair = lax.div(z, 2)
     turned = 1 - 2 * lax.rem(z, 2)
     far_first = (mod(pair + 2, 4), mod(pair + turned, 4), mod(pair - turned, 4), pair)
     n_bufs = len(bufs) // 2
+    dproj_copies = twin_weights[1:]
     delta_sum = SeqSum(
-        net, bufs[:n_bufs], delta, lambda pair: dot_nn(rows_of(mixed, pair, slice(HID, MIX)), woutp[...]), far_first
+        net, bufs[:n_bufs], delta,
+        both_cores(mixed, slice(HID, MIX), woutp, mixed2, woutp2, [twin_weights[0], mixed_copy]), far_first,
     )
     dnormed_sum = SeqSum(
-        net, bufs[n_bufs:], dnormed, lambda pair: dot_nn(rows_of(dproj, pair, slice(0, WINP)), winp[...]), far_first
+        net, bufs[n_bufs:], dnormed,
+        both_cores(dproj, slice(0, WINP), winp, dproj2, winp2, dproj_copies), far_first,
     )
-    delta_sum.multiply(False)
+    delta_sum.multiply()
     ff_ring.pass_on()
     datt_gather.done()
 
@@ -600,11 +611,11 @@
     dkey = norm_back(keyraw, key_scale, dkey_n[...] * FACTOR)
     dproj[:, :, :, HS : 2 * HS] = dkey.astype(BF16).reshape(NZ, NY, 32, HS)
     dproj[:, :, :, 2 * HS : 3 * HS] = dvalues[...].astype(BF16).reshape(NZ, NY, 32, HS)
-    delta_sum.turn()
     ff_ring.done()
-    dnormed_sum.multiply(True)
+    dproj_copies.append(net.send(dproj.at[:, :, pl.ds(twin_half, CAP)], dproj2, net.twin))
+    dnormed_sum.multiply()
     while delta_sum.turn():
-        dnormed_sum.turn()
+        pass
 
     rows = g0[z, y, c].astype(F32)
     grads = g1[z, y, c].astype(F32)
@@ -658,7 +669,6 @@
 
 def sum_scratch():
     return [
-        pltpu.VMEM((2, NZ, NY, CAP, QD), BF16),
         pltpu.VMEM((NZ, NY, CAP, QD), BF16),
         pltpu.VMEM((NY, CAP, AW), BF16),
         pltpu.VMEM((NZ, CAP, BW), BF16),
@@ -670,7 +680,7 @@
 
 
 def local(residual, chosen_pos, chosen_count, router_weight, weight_in, weight_out, cotangent):
-    n_sem = 96
+    n_sem = 95
     scratch = [
         pltpu.SemaphoreType.DMA((n_sem,)),
         pltpu.SemaphoreType.DMA((n_sem,)),
@@ -692,6 +702,10 @@
         pltpu.VMEM((NZ, NY, 32, MIX), BF16),
         pltpu.VMEM((NZ, NY, 32, HS), BF16),
         pltpu.VMEM((NZ, NY, 32, WINP), BF16),
+        pltpu.VMEM((WINP, QD), BF16),
+        pltpu.VMEM((WOUTP, QD), BF16),
+        pltpu.VMEM((NZ, NY, CAP, WOUTP), BF16),
+        pltpu.VMEM((NZ, NY, CAP, WINP), BF16),
         pltpu.VMEM((ROWS, HS), BF16),
         pltpu.VMEM((ROWS, HS), BF16),
         pltpu.VMEM((ROWS, HS), F32),

time: 140 us -> 145 us (1.036)
  Pallas kernels: 139 us -> 144 us
    pallas_call x1, Pallas kernels: 136 us -> 141 us  [local(): pl.pallas_call(kernel, out_shape=[jax.ShapeDtypeStruct((2, 4, CAP, QD), B...]
where the time goes in v6:
time: 145 us
  Pallas kernels  144 us (99%)
    pallas_call x1, Pallas kernels, local(): pl.pallas_call(kernel, out_shape=[jax.ShapeDtypeStruct((2, 4, CAP, QD), B...  141 us

profile of v6, /device:TPU:1, one launch (start us, length us, event | category | flops | bytes accessed | tf_op | source)
XLA Modules:
  0.0 145.1 jit_solution(2070313397095902465)
XLA Ops:
  1.3 141.1 %shard_map.86 = (bf16[2,4,16,2048]{3,2,1,0:T(8,128)(2,1)}, bf16[64,128]{1,0:T(8,128)(2,1)}) custom-call(s32[1,1]{1,0:T(1,128)} %bitcast.5.count_ref, s32[1,48]{1,0:T(1,128)} %bitcast.9, bf16[128,2048]{1,0:T(8,128)(2,1)} %res_ref.3, bf16[128,2048]{1,0:T(8,128)(2,1)} %cot_ref.3, f32[1,2048]{1,0:T(1,128)} %bitcast.8, bf16[832,2048]{1,0:T(8,128)(2,1)} %bitcast.7, ...), custom_call_target="tpu_custom_call" | custom-call | flops 10000000000 | bytes 10000000 | tf_op jit(solution)/shard_map/pallas_call | solution.py:720
  142.4 2.7 %shard_map.87 = (bf16[128,2048]{1,0:T(8,128)(2,1)}, bf16[128,2048]{1,0:T(8,128)(2,1)}) custom-call(bf16[64,128]{1,0:T(8,128)(2,1)} %get-tuple-element.4.sel_ref, bf16[2,64,2048]{2,1,0:T(8,128)(2,1)} %bitcast.6, bf16[128,2048]{1,0:T(8,128)(2,1)} %res_ref.3, bf16[128,2048]{1,0:T(8,128)(2,1)} %cot_ref.3), custom_call_target="tpu_custom_call" | custom-call | tf_op jit(solution)/shard_map/pallas_call | solution.py:742

commit v7 on v6

--- a/solution.py
+++ b/solution.py
@@ -611,6 +611,7 @@
     dkey = norm_back(keyraw, key_scale, dkey_n[...] * FACTOR)
     dproj[:, :, :, HS : 2 * HS] = dkey.astype(BF16).reshape(NZ, NY, 32, HS)
     dproj[:, :, :, 2 * HS : 3 * HS] = dvalues[...].astype(BF16).reshape(NZ, NY, 32, HS)
+    delta_sum.turn()
     ff_ring.done()
     dproj_copies.append(net.send(dproj.at[:, :, pl.ds(twin_half, CAP)], dproj2, net.twin))
     dnormed_sum.multiply()

time: 145 us -> 140 us (0.966)
  Pallas kernels: 144 us -> 139 us
    pallas_call x1, Pallas kernels: 141 us -> 136 us  [local(): pl.pallas_call(kernel, out_shape=[jax.ShapeDtypeStruct((2, 4, CAP, QD), B...]
where the time goes in v7:
time: 140 us
  Pallas kernels  139 us (99%)
    pallas_call x1, Pallas kernels, local(): pl.pallas_call(kernel, out_shape=[jax.ShapeDtypeStruct((2, 4, CAP, QD), B...  136 us

profile of v7, /device:TPU:1, one launch (start us, length us, event | category | flops | bytes accessed | tf_op | source)
XLA Modules:
  0.0 140.1 jit_solution(5115087295564277458)
XLA Ops:
  1.3 136.2 %shard_map.86 = (bf16[2,4,16,2048]{3,2,1,0:T(8,128)(2,1)}, bf16[64,128]{1,0:T(8,128)(2,1)}) custom-call(s32[1,1]{1,0:T(1,128)} %bitcast.5.count_ref, s32[1,48]{1,0:T(1,128)} %bitcast.9, bf16[128,2048]{1,0:T(8,128)(2,1)} %res_ref.3, bf16[128,2048]{1,0:T(8,128)(2,1)} %cot_ref.3, f32[1,2048]{1,0:T(1,128)} %bitcast.8, bf16[832,2048]{1,0:T(8,128)(2,1)} %bitcast.7, ...), custom_call_target="tpu_custom_call" | custom-call | flops 10000000000 | bytes 10000000 | tf_op jit(solution)/shard_map/pallas_call | solution.py:721
  137.4 2.7 %shard_map.87 = (bf16[128,2048]{1,0:T(8,128)(2,1)}, bf16[128,2048]{1,0:T(8,128)(2,1)}) custom-call(bf16[64,128]{1,0:T(8,128)(2,1)} %get-tuple-element.4.sel_ref, bf16[2,64,2048]{2,1,0:T(8,128)(2,1)} %bitcast.6, bf16[128,2048]{1,0:T(8,128)(2,1)} %res_ref.3, bf16[128,2048]{1,0:T(8,128)(2,1)} %cot_ref.3), custom_call_target="tpu_custom_call" | custom-call | tf_op jit(solution)/shard_map/pallas_call | solution.py:743

commit v8 on v7

--- a/solution.py
+++ b/solution.py
@@ -19,7 +19,7 @@
 ROWS = 1024
 BLK = 256
 HALF = QD // 2
-AW = 512
+AW = 768
 BW = QD - AW
 MIX = 2 * WOUTP
 HID = 3 * HS
@@ -185,11 +185,42 @@
         arrive(self.copy)
 
 
+def chain(net, block, from_left, from_right):
+    hops, half = NZ // 2, AW // 2
+    far = mod(net.z + hops, NZ)
+    copy = net.group(
+        [
+            (block(far, 0, half), from_left.at[0, ..., 0:half], net.zp),
+            (block(far, half, AW), from_right.at[0, ..., half:AW], net.zm),
+        ],
+        from_left.at[0],
+    )
+    yield
+    for step in range(1, hops):
+        right, left = mod(net.z + hops - step, NZ), mod(net.z - hops + step, NZ)
+        arrive(copy)
+        for at, landed, (lo, hi) in ((right, from_left, (0, half)), (left, from_right, (half, AW))):
+            if step > 1:
+                lo, hi = 0, AW
+            target = block(at, lo, hi)
+            target[...] = (target[...].astype(F32) + landed[step - 1, ..., lo:hi].astype(F32)).astype(BF16)
+        copy = net.group(
+            [
+                (block(right, 0, AW), from_left.at[step], net.zp),
+                (block(left, 0, AW), from_right.at[step], net.zm),
+            ],
+            from_left.at[0:2],
+        )
+        yield
+    arrive(copy)
+
+
 class SeqSum:
     def __init__(self, net, bufs, out, product, order):
         self.net, self.out, self.product, self.order = net, out, product, order
-        self.part, self.qa, self.qb, self.azl, self.ayl, self.byl, self.bzl = bufs
-        self.along_z_a, self.along_z_b = net.open(), net.open()
+        self.part, self.qa, self.qb, self.azl, self.azr, self.ayl, self.byl, self.bzl = bufs
+        self.along_z_b = net.open()
+        self.ring = chain(net, lambda t, lo, hi: self.part.at[t, :, :, lo:hi], self.azl, self.azr)
         self.along_y_b = []
         self.steps = self.finish()
 
@@ -211,11 +242,11 @@
                         at = ((i * 2 + place) * NY + y) * CAP
                         self.part[2 * pair + place, y] = rows[at : at + CAP].astype(BF16)
                 self.send(2 * half + i)
+            if half == 0:
+                self.pass_on()
 
     def send(self, k):
         net, part = self.net, self.part
-        for z in self.places(k)[1]:
-            net.put(self.along_z_a, part.at[z, :, :, 0:AW], self.azl.at[net.z], self.at_z(z))
         rows = pl.ds(2 * self.order[k], 2)
         copies = [
             (part.at[rows, mod(net.y + d, NY), :, AW:QD], self.byl.at[d - 1, rows], net.along_y[d - 1])
@@ -235,17 +266,25 @@
         for z in others:
             net.put(self.along_z_b, self.qb.at[z], self.bzl.at[net.z], self.at_z(z))
 
+    def pass_on(self):
+        next(self.ring, None)
+
     def turn(self):
         return next(self.steps, None) is not None
 
     def finish(self):
         net = self.net
-        for k in range(4):
-            self.sum_y(k)
-        arrive(net.close(self.along_z_a, self.azl.at[0 : NZ - 1]))
-        total = self.part[net.z, :, :, 0:AW].astype(F32)
-        for d in range(1, NZ):
-            total = total + self.azl[mod(net.z + d, NZ)].astype(F32)
+        self.pass_on()
+        self.sum_y(0)
+        self.pass_on()
+        self.sum_y(1)
+        self.sum_y(2)
+        self.pass_on()
+        self.sum_y(3)
+        for _ in self.ring:
+            pass
+        last = NZ // 2 - 1
+        total = self.part[net.z, :, :, 0:AW].astype(F32) + self.azl[last].astype(F32) + self.azr[last].astype(F32)
         self.qa[...] = total.astype(BF16)
         copy = net.group(
             [(self.qa.at[mod(net.y + d, NY)], self.ayl.at[d - 1], net.along_y[d - 1]) for d in range(1, NY)], self.ayl
@@ -586,6 +625,7 @@
     delta_sum.multiply()
     ff_ring.pass_on()
     datt_gather.done()
+    delta_sum.pass_on()
 
     def norm_back(values, scale, grads):
         return scale * grads - values * scale**3 * jnp.mean(grads * values, axis=-1, keepdims=True)
@@ -608,6 +648,8 @@
         else:
             dkey_n[0:last] = dkey_n[0:last] + dkey_part
             dvalues[0:last] = dvalues[0:last] + dvalue_part
+        if block == 3 or block == 1:
+            delta_sum.pass_on()
     dkey = norm_back(keyraw, key_scale, dkey_n[...] * FACTOR)
     dproj[:, :, :, HS : 2 * HS] = dkey.astype(BF16).reshape(NZ, NY, 32, HS)
     dproj[:, :, :, 2 * HS : 3 * HS] = dvalues[...].astype(BF16).reshape(NZ, NY, 32, HS)
@@ -673,7 +715,8 @@
         pltpu.VMEM((NZ, NY, CAP, QD), BF16),
         pltpu.VMEM((NY, CAP, AW), BF16),
         pltpu.VMEM((NZ, CAP, BW), BF16),
-        pltpu.VMEM((NZ, NY, CAP, AW), BF16),
+        pltpu.VMEM((NZ // 2, NY, CAP, AW), BF16),
+        pltpu.VMEM((NZ // 2, NY, CAP, AW), BF16),
         pltpu.VMEM((NY - 1, CAP, AW), BF16),
         pltpu.VMEM((NY - 1, NZ, CAP, BW), BF16),
         pltpu.VMEM((NZ, CAP, BW), BF16),
@@ -681,7 +724,7 @@
 
 
 def local(residual, chosen_pos, chosen_count, router_weight, weight_in, weight_out, cotangent):
-    n_sem = 95
+    n_sem = 101
     scratch = [
         pltpu.SemaphoreType.DMA((n_sem,)),
         pltpu.SemaphoreType.DMA((n_sem,)),

time: 140 us -> 146 us (1.043); the launches traced: 140 us -> 144 us
  Pallas kernels: 139 us -> 143 us
    pallas_call x1, Pallas kernels: 136 us -> 140 us  [local(): pl.pallas_call(kernel, out_shape=[jax.ShapeDtypeStruct((2, 4, CAP, QD), B...]
where the time goes in v8:
time: 146 us; the launch traced here: 144 us
  Pallas kernels  143 us (98%)
    pallas_call x1, Pallas kernels, local(): pl.pallas_call(kernel, out_shape=[jax.ShapeDtypeStruct((2, 4, CAP, QD), B...  140 us

profile of v8, /device:TPU:1, one launch (start us, length us, event | category | flops | bytes accessed | tf_op | source)
XLA Modules:
  0.0 144.3 jit_solution(8907657921520497326)
XLA Ops:
  1.3 140.3 %shard_map.86 = (bf16[2,4,16,2048]{3,2,1,0:T(8,128)(2,1)}, bf16[64,128]{1,0:T(8,128)(2,1)}) custom-call(s32[1,1]{1,0:T(1,128)} %bitcast.5.count_ref, s32[1,48]{1,0:T(1,128)} %bitcast.9, bf16[128,2048]{1,0:T(8,128)(2,1)} %res_ref.3, bf16[128,2048]{1,0:T(8,128)(2,1)} %cot_ref.3, f32[1,2048]{1,0:T(1,128)} %bitcast.8, bf16[832,2048]{1,0:T(8,128)(2,1)} %bitcast.7, ...), custom_call_target="tpu_custom_call" | custom-call | flops 10000000000 | bytes 10000000 | tf_op jit(solution)/shard_map/pallas_call | solution.py:764
  141.6 2.7 %shard_map.87 = (bf16[128,2048]{1,0:T(8,128)(2,1)}, bf16[128,2048]{1,0:T(8,128)(2,1)}) custom-call(bf16[64,128]{1,0:T(8,128)(2,1)} %get-tuple-element.4.sel_ref, bf16[2,64,2048]{2,1,0:T(8,128)(2,1)} %bitcast.6, bf16[128,2048]{1,0:T(8,128)(2,1)} %res_ref.3, bf16[128,2048]{1,0:T(8,128)(2,1)} %cot_ref.3), custom_call_target="tpu_custom_call" | custom-call | tf_op jit(solution)/shard_map/pallas_call | solution.py:786

commit v9 on v7

--- a/solution.py
+++ b/solution.py
@@ -584,7 +584,6 @@
         both_cores(dproj, slice(0, WINP), winp, dproj2, winp2, dproj_copies), far_first,
     )
     delta_sum.multiply()
-    ff_ring.pass_on()
     datt_gather.done()
 
     def norm_back(values, scale, grads):
@@ -608,6 +607,8 @@
         else:
             dkey_n[0:last] = dkey_n[0:last] + dkey_part
             dvalues[0:last] = dvalues[0:last] + dvalue_part
+        if block == 2:
+            ff_ring.pass_on()
     dkey = norm_back(keyraw, key_scale, dkey_n[...] * FACTOR)
     dproj[:, :, :, HS : 2 * HS] = dkey.astype(BF16).reshape(NZ, NY, 32, HS)
     dproj[:, :, :, 2 * HS : 3 * HS] = dvalues[...].astype(BF16).reshape(NZ, NY, 32, HS)

time: 140 us -> 140 us (level)
  no operation moved by 1% of the time
where the time goes in v9:
time: 140 us
  Pallas kernels  139 us (99%)
    pallas_call x1, Pallas kernels, local(): pl.pallas_call(kernel, out_shape=[jax.ShapeDtypeStruct((2, 4, CAP, QD), B...  136 us

profile of v9, /device:TPU:1, one launch (start us, length us, event | category | flops | bytes accessed | tf_op | source)
XLA Modules:
  0.0 140.1 jit_solution(9857307323796012972)
XLA Ops:
  1.3 136.2 %shard_map.86 = (bf16[2,4,16,2048]{3,2,1,0:T(8,128)(2,1)}, bf16[64,128]{1,0:T(8,128)(2,1)}) custom-call(s32[1,1]{1,0:T(1,128)} %bitcast.5.count_ref, s32[1,48]{1,0:T(1,128)} %bitcast.9, bf16[128,2048]{1,0:T(8,128)(2,1)} %res_ref.3, bf16[128,2048]{1,0:T(8,128)(2,1)} %cot_ref.3, f32[1,2048]{1,0:T(1,128)} %bitcast.8, bf16[832,2048]{1,0:T(8,128)(2,1)} %bitcast.7, ...), custom_call_target="tpu_custom_call" | custom-call | flops 10000000000 | bytes 10000000 | tf_op jit(solution)/shard_map/pallas_call | solution.py:722
  137.4 2.7 %shard_map.87 = (bf16[128,2048]{1,0:T(8,128)(2,1)}, bf16[128,2048]{1,0:T(8,128)(2,1)}) custom-call(bf16[64,128]{1,0:T(8,128)(2,1)} %get-tuple-element.4.sel_ref, bf16[2,64,2048]{2,1,0:T(8,128)(2,1)} %bitcast.6, bf16[128,2048]{1,0:T(8,128)(2,1)} %res_ref.3, bf16[128,2048]{1,0:T(8,128)(2,1)} %cot_ref.3), custom_call_target="tpu_custom_call" | custom-call | tf_op jit(solution)/shard_map/pallas_call | solution.py:744
